TPU v7x, 256 devices: a whole 4x4x8 slice. The times are simulated.
256 devices in a mesh: freq: 128 (over z, x, y_lo, core), tile: 2 (over y_hi).
Axes of the slice: x: 4, y: 4 (y_hi: 2, y_lo: 2; y = y_hi * 2 + y_lo), z: 8, core: 2. Of those that a mesh axis runs over, the one named last changes fastest.
Arguments:
- source_field: float32 [2, 128, 128, 1024], P(None, 'freq', 'tile'), may hold values from -6 to 6
- receiver_field: float32 [2, 128, 128, 1024], P(None, 'freq', 'tile'), may hold values from -6 to 6
- omegas: float32 [128], P('freq'), may hold values from 30 to 380
- velocity: float32 [256, 128, 1024], P('freq', 'tile'), may hold values from 1500 to 4500
- epsilon: float32 [256, 128, 1024], P('freq', 'tile'), may hold values from 0 to 0.3
- delta: float32 [256, 128, 1024], P('freq', 'tile'), may hold values from -0.1 to 0.2
- owner_map: int32 [256], replicated, may hold values from 0 to 255, each once
- stencil_reach: int32 [2], replicated, may hold values from 1 to 3, as said below
- source_rows: int32 [4], replicated, may hold values from 0 to 127
- source_cols: int32 [4], replicated, may hold values from 0 to 1023
Outputs:
- source_next: float32 [2, 128, 128, 1024], P(None, 'freq', 'tile')
- receiver_next: float32 [2, 128, 128, 1024], P(None, 'freq', 'tile')
- image: float32 [2, 128, 1024], P(None, 'tile')
Inputs may be any that keep to these rules, and one draw needn't show every extreme that they name: `stencil_reach`: some step has half-width 3.
All inputs are finite; a program needn't handle non-finite values.
Results may differ from a plain program's by a relative error of at most 0.0002.
Values sent between devices are 32-bit elements; how exact they have to be, the bound alone decides.
A program may use at most 64 MiB of HBM per device.

v0:
```python
import math

import jax
import jax.numpy as jnp
from jax import lax
from jax.sharding import PartitionSpec as P

STEPS = 2
HMAX = 3


depth_step = 10.0
lateral_step = 10.0
source_delay = 0.05
source_amplitude = 16.0
image_gain = 16.0
taper_width = 4.0


def broadcast(block, axis, source):
    block = jnp.where(lax.axis_index(axis) == source, block, jnp.zeros_like(block))
    return lax.psum(block, axis)


def with_halo(block, sides, width):
    for axis, dim in sides:
        count = lax.axis_size(axis)
        forward = [(i, i + 1) for i in range(count - 1)]
        backward = [(target, source) for source, target in forward]
        low = lax.ppermute(
            lax.slice_in_dim(block, block.shape[dim] - width, None, axis=dim), axis, forward
        )
        high = lax.ppermute(lax.slice_in_dim(block, 0, width, axis=dim), axis, backward)
        block = jnp.concatenate([low, block, high], axis=dim)
    return block


def offset_groups(half_width):
    offsets_range = range(-half_width, half_width + 1)
    radii = sorted(
        set(
            (
                down_shift * down_shift + side_shift * side_shift
                for down_shift in offsets_range
                for side_shift in offsets_range
            )
        )
    )
    return [
        (
            radius,
            [
                (down_shift, side_shift)
                for down_shift in offsets_range
                for side_shift in offsets_range
                if down_shift * down_shift + side_shift * side_shift == radius
            ],
        )
        for radius in radii
    ]


def step_weights(reach_now, groups):
    tapers = jnp.array([math.exp(-radius / taper_width) for radius, members in groups], jnp.float32)
    counts = jnp.array([len(members) for radius, members in groups], jnp.float32)
    needed = jnp.array(
        [
            max((max(abs(down_shift), abs(side_shift)) for down_shift, side_shift in members))
            for radius, members in groups
        ],
        jnp.int32,
    )
    live_mask = (needed <= reach_now).astype(jnp.float32)
    normalizer = jnp.sum(tapers * counts * live_mask)
    return tapers * live_mask / normalizer


def inject(fields, omegas, source_spots):
    delay_phase = omegas * source_delay
    pulse_real = (source_amplitude * jnp.cos(delay_phase))[:, None, None] * source_spots[None]
    pulse_imag = (-source_amplitude * jnp.sin(delay_phase))[:, None, None] * source_spots[None]
    return jnp.concatenate(
        [fields[0:1] + pulse_real[None], fields[1:2] + pulse_imag[None], fields[2:4]], axis=0
    )


def extrapolate(padded, omegas, planes, weights, groups):
    row_count = padded.shape[2] - 2 * HMAX
    col_count = padded.shape[3] - 2 * HMAX
    velocity_now, epsilon_now, delta_now = (planes[0], planes[1], planes[2])
    stretch = 1.0 / (1.0 + 2.0 * delta_now)
    slowness = 1.0 / velocity_now
    vert_wave = omegas[:, None, None] * (depth_step * slowness)[None]
    curvature = (
        omegas[:, None, None]
        * (lateral_step * lateral_step / (2.0 * depth_step) * slowness * stretch)[None]
    )
    eta_ratio = ((epsilon_now - delta_now) * stretch)[None]
    summed = jnp.zeros((4, padded.shape[1], row_count, col_count), jnp.float32)
    for group_index, (radius, members) in enumerate(groups):
        gathered = None
        for down_shift, side_shift in members:
            piece = padded[
                :,
                :,
                HMAX + down_shift : HMAX + down_shift + row_count,
                HMAX + side_shift : HMAX + side_shift + col_count,
            ]
            gathered = piece if gathered is None else gathered + piece
        phase_angle = vert_wave + curvature * radius * (1.0 - eta_ratio * (radius / 8.0))
        weight_real = weights[group_index] * jnp.cos(phase_angle)
        weight_imag = weights[group_index] * jnp.sin(phase_angle)
        summed = summed + jnp.stack(
            [
                weight_real * gathered[0] - weight_imag * gathered[1],
                weight_real * gathered[1] + weight_imag * gathered[0],
                weight_real * gathered[2] + weight_imag * gathered[3],
                weight_real * gathered[3] - weight_imag * gathered[2],
            ]
        )
    return summed


def correlate(fields):
    return jnp.sum(fields[0] * fields[2] + fields[1] * fields[3], axis=0)


def per_device(
    source_field,
    receiver_field,
    omegas,
    velocity,
    epsilon,
    delta,
    owner_map,
    stencil_reach,
    source_rows,
    source_cols,
):
    groups = offset_groups(HMAX)
    row_count = source_field.shape[2]
    col_count = source_field.shape[3]
    slab_count = velocity.shape[0]
    global_rows = lax.axis_index("tile") * row_count + jnp.arange(row_count, dtype=jnp.int32)
    row_hit = (source_rows[None, :] == global_rows[:, None]).astype(jnp.float32)
    col_hit = (source_cols[:, None] == jnp.arange(col_count, dtype=jnp.int32)[None, :]).astype(
        jnp.float32
    )
    source_spots = jnp.dot(
        row_hit, col_hit, precision=lax.Precision.HIGHEST, preferred_element_type=jnp.float32
    )
    fields = jnp.concatenate([source_field, receiver_field], axis=0)
    fields = inject(fields, omegas, source_spots)
    images = []
    for depth_index in range(STEPS):
        model_row = owner_map[depth_index]
        owner_root = model_row // slab_count
        owner_slot = model_row % slab_count
        mine = jnp.stack([velocity[owner_slot], epsilon[owner_slot], delta[owner_slot]])
        owner_root, mine = (owner_root, mine)
        planes = broadcast(mine, "freq", owner_root)
        padded = with_halo(fields, (("tile", 2),), HMAX)
        padded = jnp.pad(padded, ((0, 0), (0, 0), (0, 0), (HMAX, HMAX)))
        fields = extrapolate(
            padded, omegas, planes, step_weights(stencil_reach[depth_index], groups), groups
        )
        image_term = correlate(fields)
        images.append(lax.psum(image_term, "freq"))
    image = jnp.stack(images)
    image = image * (image_gain / math.sqrt(omegas.shape[0] * lax.axis_size("freq")))
    return (fields[0:2], fields[2:4], image)


def solution(mesh):
    in_specs = (
        P(None, "freq", "tile", None),
        P(None, "freq", "tile", None),
        P("freq"),
        P("freq", "tile", None),
        P("freq", "tile", None),
        P("freq", "tile", None),
        P(),
        P(),
        P(),
        P(),
    )
    out_specs = (
        P(None, "freq", "tile", None),
        P(None, "freq", "tile", None),
        P(None, "tile", None),
    )
    return jax.shard_map(
        per_device, mesh=mesh, in_specs=in_specs, out_specs=out_specs, check_vma=False
    )
```

profile of v0, /device:TPU:1, one launch (start us, length us, event | category | flops | bytes accessed | tf_op | source)
XLA Modules:
  0.0 2181.9 jit_solution(13816985890351998888)
XLA Ops:
  8.1 1.3 bitcast_add_fusion.1
  9.4 1.0 pad_maximum_fusion.5
  10.4 5.8 collective-permute-start
  16.2 1.3 collective-permute-start.1
  23.5 1.0 maximum_select_fusion
  24.5 0.9 maximum_select_fusion.1
  26.1 2.0 fusion.54
  28.1 2.7 fusion.53
  32.9 3.6 slice_add_fusion.49
  36.5 5.2 slice_add_fusion.35
  41.7 5.2 slice_add_fusion.42
  46.9 1030.1 %all-reduce.9.cloned.1.call-done = (f32[3,64,1024]{2,1,0:T(8,128)}, f32[3,64,1024]{2,1,0:T(8,128)}) async-done(((f32[3,64,1024]{2,1,0:T(8,128)}, f32[3,64,1024]{2,1,0:T(8,128)}), (f32[3,64,1024]{2,1,0:T(8,128)}, f32[3,64,1024]{2,1,0:T(8,128)})) %all-reduce.9.cloned.1.call-update) | async-done | bytes 1572880 | tf_op jit(solution)/shard_map/psum | solution.py:22
  1077.0 3.6 subtract_bitcast_fusion.19
  1080.6 2.7 fusion.45
  1083.3 7.6 subtract_bitcast_fusion.21
  1091.0 3.4 add_bitcast_fusion.20
  1094.5 3.5 add_bitcast_fusion.22
  1098.0 7.4 subtract_bitcast_fusion.29
  1105.4 3.4 add_bitcast_fusion.24
  1108.8 3.3 add_bitcast_fusion.32
  1112.1 3.4 fusion.41
  1115.5 1.3 fusion.19
  1116.9 4.4 collective-permute-start.2
  1121.3 1.5 collective-permute-start.3
  1122.8 0.8 add_bitcast_fusion
  1123.5 4.3 collective-permute-done.3
  1128.9 3.8 slice_add_fusion.3
  1132.8 3.9 slice_add_fusion.10
  1136.7 2.0 subtract_bitcast_fusion.1
  1138.6 1.7 add_bitcast_fusion.2
  1140.3 1.5 fusion.11
  1141.9 6.6 subtract_bitcast_fusion.3
  1148.4 1.6 add_bitcast_fusion.4
  1150.0 1.7 add_bitcast_fusion.6
  1151.8 1.7 add_bitcast_fusion.8
  1153.5 1.7 add_bitcast_fusion.10
  1155.2 6.4 subtract_bitcast_fusion.11
  1161.6 1.7 add_bitcast_fusion.12
  1163.3 1.6 add_bitcast_fusion.14
  1164.9 1.6 add_bitcast_fusion.16
  1166.6 1.7 add_bitcast_fusion.18
  1168.3 1.7 fusion.37
  1170.0 1.7 fusion.39
  1171.7 1.3 fusion.27
  1173.0 0.8 fusion.29
  1173.8 1.0 fusion.59
  1174.8 998.1 %all-reduce.7.cloned.1.call-done = (f32[1,64,1024]{2,1,0:T(8,128)}, f32[1,64,1024]{2,1,0:T(8,128)}) async-done(((f32[1,64,1024]{2,1,0:T(8,128)}, f32[1,64,1024]{2,1,0:T(8,128)}), (f32[1,64,1024]{2,1,0:T(8,128)}, f32[1,64,1024]{2,1,0:T(8,128)})) %all-reduce.7.cloned.1.call-update) | async-done | bytes 524304 | tf_op jit(solution)/shard_map/psum | solution.py:168
  2172.9 1.9 maximum_multiply_fusion
  (54 shorter events, 4.7 us)
Async XLA Ops:
  7.2 10.3 copy-start.14
  7.2 16.1 copy-start.9
  7.2 1069.8 %all-reduce.9.cloned.1.call-start = ((), (), s32[]{:S(2)}) async-start(), calls=%async_computation.1 | async-start | bytes 3145728 | tf_op jit(solution)/shard_map/psum | solution.py:22
  9.4 14.0 copy-start.10
  10.4 13.0 copy-start.11
  10.4 21.8 collective-permute-start
  16.2 16.0 collective-permute-start.1
  24.5 1.0 copy-start.12
  24.5 1.6 copy-start.13
  24.5 1.6 copy-start.15
  24.5 3.6 copy-start.16
  24.5 7.7 copy-start
  25.5 2147.4 %all-reduce.7.cloned.1.call-start = ((), (), s32[]{:S(2)}) async-start(), calls=%async_computation | async-start | bytes 1048576 | tf_op jit(solution)/shard_map/psum | solution.py:168
  1077.0 6.3 copy-start.4
  1077.0 6.3 copy-start.5
  1077.0 6.3 copy-start.6
  1080.6 2.7 copy-start.2
  1083.3 7.6 copy-start.7
  1094.4 3.5 copy-start.1
  1094.4 3.5 copy-start.3
  1116.9 6.6 collective-permute-start.2
  1121.3 6.5 collective-permute-start.3
  1132.8 3.9 copy-start.8
Sparse Core Ops, SparseCore 0:
  25.6 1051.3 all-reduce.8
  1173.9 998.9 all-reduce.6
where the time goes:
time: 2190 us; the launch traced here: 2180 us
  waiting for transfers between devices  2030 us (93%)
  other arithmetic  110 us (5%)
    psum x1, waiting for transfers between devices, broadcast(): return lax.psum(block, axis)  1030 us
    psum x1, waiting for transfers between devices, per_device(): images.append(lax.psum(image_term, 'freq'))  998 us
    another operation x23, other arithmetic, extrapolate(): jnp.stack([weight_real * gathered[0] - weight_imag * gathered[1], weight_...  71.7 us
  transfers between devices with their start and end apart: 6, of which 3 were waited for; matrix products, arithmetic and copies ran while one was open for 1% of the time, Pallas kernels for 0%

commit v1 on v0

v1 whole, which is shorter than its diff:
```python
import math

import jax
import jax.numpy as jnp
import numpy as np
from jax import lax
from jax.experimental import pallas as pl
from jax.experimental.pallas import tpu as pltpu
from jax.sharding import PartitionSpec as P

STEPS = 2
HMAX = 3
ROWS = 64
TALL = ROWS + 2 * HMAX
LANES = 128
GAIN = 16.0 / math.sqrt(128.0)
MESH = pl.DeviceIdType.MESH
F32 = jnp.float32


def _minimax(fn, high, degree, weight):
    count = 2000
    nodes = high / 2 + high / 2 * np.cos(np.pi * (np.arange(count) + 0.5) / count)
    target, scale = fn(nodes), weight(nodes)
    table = np.vander(nodes, degree + 1, increasing=True)
    bias = np.ones(count)
    best, least = None, np.inf
    for _ in range(60):
        coefs = np.linalg.lstsq(table * (bias * scale)[:, None], target * bias * scale, rcond=None)[0]
        error = np.abs((table @ coefs - target) * scale)
        if error.max() < least:
            best, least = coefs, error.max()
        bias = bias * (error / error.max() + 1e-3) ** 0.3
        bias = bias / bias.max()
    return tuple(float(np.float32(c)) for c in best)


REACH_SQ = 1.6 * 1.6
SIN = _minimax(lambda u: np.sin(np.sqrt(u)) / np.sqrt(u), REACH_SQ, 4, np.sqrt)
COS = _minimax(lambda u: np.cos(np.sqrt(u)), REACH_SQ, 4, np.ones_like)

GROUPS = sorted({a * a + b * b for a in range(4) for b in range(4)})
COUNTS = [
    sum(1 for a in range(-3, 4) for b in range(-3, 4) if a * a + b * b == r) for r in GROUPS
]
NEEDED = [
    max(max(a, b) for a in range(4) for b in range(4) if a * a + b * b == r) for r in GROUPS
]
TAPERS = [float(np.float32(math.exp(-r / 4.0))) for r in GROUPS]


def at(unit, count=1):
    return pl.ds(pl.multiple_of(unit * 8, 8), count * 8)


def horner(u, coefs):
    value = coefs[-1] * u + coefs[-2]
    for c in coefs[-3::-1]:
        value = value * u + c
    return value


def cis(x):
    u = x * x
    return horner(u, COS), x * horner(u, SIN)


def mul(a, b):
    return a[0] * b[0] - a[1] * b[1], a[0] * b[1] + a[1] * b[0]


def square(a):
    twice = a[1] + a[1]
    return 1.0 - a[1] * twice, a[0] * twice


def coords():
    f = lax.axis_index("freq")
    return f // 16, (f // 4) % 4, (f // 2) % 2, f % 2


def device(z, x, y, c):
    return {"freq": ((z * 4 + x) * 2 + y) * 2 + c}


def xy_peers():
    z, x, y, c = coords()
    out = []
    for k in range(1, 8):
        px, py = (x + k // 2) % 4, (y + k % 2) % 2
        out.append((device(z, px, py, c), px * 2 + py))
    return x * 2 + y, out


def z_peers():
    z, x, y, c = coords()
    return z, [(device((z + k) % 8, x, y, c), (z + k) % 8) for k in range(1, 8)]


def core_peer():
    z, x, y, c = coords()
    return device(z, x, y, 1 - c)


def all_peers():
    return [core_peer()] + [d for d, _ in xy_peers()[1]] + [d for d, _ in z_peers()[1]]


class Stream:
    SEMS = 30

    def __init__(self, src, res, base, units, order, bufs, sends, recvs):
        self.src, self.res, self.base, self.units = src, res, base, units
        self.core_in, self.half, self.in1, self.sum1, self.in2, self.out1 = bufs
        self.sends, self.recvs = sends, recvs
        self.groups = [xy_peers() if o == "xy" else z_peers() for o in order]
        self.core = coords()[3]
        self.started = []

    @staticmethod
    def scratch(units):
        def block(n):
            return pltpu.VMEM((n * 8, LANES), F32)

        return [
            block(units // 2),
            block(units // 2),
            block(7 * units // 16),
            block(units // 16),
            block(7 * units // 128),
            block(units // 16),
        ]

    def copy(self, slot, src, dst, to):
        made = pltpu.make_async_remote_copy(
            src_ref=src,
            dst_ref=dst,
            send_sem=self.sends.at[slot],
            recv_sem=self.recvs.at[slot],
            device_id=to,
            device_id_type=MESH,
        )
        made.start()
        self.started.append(made)
        return made

    def core_out(self):
        n = self.units // 2
        other = self.base + (1 - self.core) * n
        self.flying = [self.copy(0, self.src.at[at(other, n)], self.core_in, core_peer())]

    def land(self):
        for made in self.flying:
            made.wait_recv()

    def core_sum(self):
        n = self.units // 2
        mine = self.base + self.core * n

        def body(i, _):
            self.half[at(i * 4, 4)] = self.src[at(mine + i * 4, 4)] + self.core_in[at(i * 4, 4)]
            return 0

        lax.fori_loop(0, n // 4, body, 0)

    def scatter1(self):
        n = self.units // 16
        self.flying = [
            self.copy(1 + k, self.half.at[at(j * n, n)], self.in1.at[at(k * n, n)], to)
            for k, (to, j) in enumerate(self.groups[0][1])
        ]

    def sum1_(self):
        n = self.units // 16
        me = self.groups[0][0]

        def body(i, _):
            total = self.half[at(me * n + i)]
            for k in range(7):
                total = total + self.in1[at(k * n + i)]
            self.sum1[at(i)] = total
            return 0

        lax.fori_loop(0, n, body, 0)

    def scatter2(self):
        n = self.units // 128
        self.flying = [
            self.copy(8 + k, self.sum1.at[at(j * n, n)], self.in2.at[at(k * n, n)], to)
            for k, (to, j) in enumerate(self.groups[1][1])
        ]

    def sum2_(self):
        n = self.units // 128
        me = self.groups[1][0]
        for i in range(n):
            total = self.sum1[at(me * n + i)]
            for k in range(7):
                total = total + self.in2[at(k * n + i)]
            self.out1[at(me * n + i)] = total

    def gather2(self):
        n = self.units // 128
        me = self.groups[1][0]
        self.flying = [
            self.copy(15 + k, self.out1.at[at(me * n, n)], self.out1.at[at(me * n, n)], to)
            for k, (to, j) in enumerate(self.groups[1][1])
        ]

    def gather1(self):
        n = self.units // 16
        place = self.base + self.core * (self.units // 2) + self.groups[0][0] * n
        self.flying = [
            self.copy(22 + k, self.out1, self.res.at[at(place, n)], to)
            for k, (to, j) in enumerate(self.groups[0][1])
        ]

        def body(i, _):
            self.res[at(place + i)] = self.out1[at(i)]
            return 0

        lax.fori_loop(0, n, body, 0)

    def core_back(self):
        n = self.units // 2
        mine = self.base + self.core * n
        self.flying = [
            self.copy(29, self.res.at[at(mine, n)], self.res.at[at(mine, n)], core_peer())
        ]

    def finish(self):
        for made in self.started:
            made.wait_send()


def reduce_all(streams):
    for s in streams:
        s.core_out()
    for s in streams:
        s.land()
        s.core_sum()
        s.scatter1()
    for s in streams:
        s.land()
        s.sum1_()
        s.scatter2()
    for s in streams:
        s.land()
        s.sum2_()
        s.gather2()
    for s in streams:
        s.land()
        s.gather1()
    for s in streams:
        s.land()
        s.core_back()


def spread(field, pairs):
    def body(i, _):
        lane = lax.broadcasted_iota(jnp.int32, (8, LANES), 1)
        block = lax.broadcasted_iota(jnp.int32, (8, LANES), 0)
        for c in range(4):
            here = field[at(i * 4 + c)]
            above = jnp.where(block < 7, pltpu.roll(here, 7, 0), 0.0)
            below = jnp.where(block > 0, pltpu.roll(here, 1, 0), 0.0)
            for b in range(1, 4):
                plus = pltpu.roll(jnp.where(lane < b, above, here), LANES - b, 1)
                minus = pltpu.roll(jnp.where(lane >= LANES - b, below, here), b, 1)
                pairs[b - 1][at(i * 4 + c)] = plus + minus
        return 0

    return body


def weights_of(planes, step, x, omega):
    t, s = x // 8, x % 8

    def row(array):
        start = (step * 3 + array) * 512 + t * 64 + s
        return planes[pl.ds(start, 8, stride=8)]

    turn = cis((0.5 * omega) * row(0))
    turn = square(turn)
    q, a = omega * row(1), omega * row(2)
    z = cis(q)
    u = a * a
    w1 = (1.0 + u * (-0.5 + u * (1.0 / 24.0)), a * (u * (1.0 / 6.0) - 1.0))
    w2 = square(w1)
    w4 = square(w2)
    w8 = square(w4)
    w16 = square(w8)
    w32 = square(w16)
    w64 = square(w32)
    w128 = square(w64)
    g = {}
    g[1] = mul(z, w1)
    g[2] = mul(square(g[1]), w2)
    g[4] = mul(square(g[2]), w8)
    g[8] = mul(square(g[4]), w32)
    g[5] = mul(mul(g[4], w8), g[1])
    g[9] = mul(mul(g[8], w16), g[1])
    w34 = mul(w32, w2)
    g[10] = mul(square(g[5]), mul(w34, w16))
    g[13] = mul(mul(g[9], g[4]), mul(w64, w8))
    g[18] = mul(square(g[9]), mul(w34, w128))
    return turn, g


def one_row(field, pairs, planes, coef, step, x, omega):
    rows = [field] + list(pairs)

    def gathered(r, c):
        total = None
        for a in range(4):
            for b in range(4):
                if a * a + b * b != r:
                    continue
                for shift in sorted({a, -a}):
                    piece = rows[b][at((x + HMAX + shift) * 4 + c)]
                    total = piece if total is None else total + piece
        return total

    turn, g = weights_of(planes, step, x, omega)
    first = coef[at(step * 10)]
    acc = [first * gathered(0, c) for c in range(4)]
    for index, r in enumerate(GROUPS):
        if r == 0:
            continue
        scale = coef[at(step * 10 + index)]
        wr, wi = g[r][0] * scale, g[r][1] * scale
        sr, si, rr, ri = [gathered(r, c) for c in range(4)]
        acc[0] = acc[0] + (wr * sr - wi * si)
        acc[1] = acc[1] + (wr * si + wi * sr)
        acc[2] = acc[2] + (wr * rr + wi * ri)
        acc[3] = acc[3] + (wr * ri - wi * rr)
    tr, ti = turn
    return (
        tr * acc[0] - ti * acc[1],
        tr * acc[1] + ti * acc[0],
        tr * acc[2] + ti * acc[3],
        tr * acc[3] - ti * acc[2],
    )


PLANE_UNITS = STEPS * 3 * ROWS
IMAGE_UNITS = STEPS * ROWS


def kernel(
    omegas, owner, reach, srows, scols, source, receiver, velocity, epsilon, delta,
    source_out, receiver_out, image_out,
    raw_fields, raw_model, cand, planes, field0, field1, field2, pair1, pair2, pair3, coef, images,
    image_sum, image_nat, load_sems, halo_sends, halo_recvs, a_sends, a_recvs, b_sends, b_recvs,
    i_sends, i_recvs, *stream_bufs,
):
    tile = lax.axis_index("tile")
    index = lax.axis_index("freq")
    neighbour = {"tile": 1 - tile}
    omega = omegas[0]
    pairs = (pair1, pair2, pair3)

    loads = []
    for i, array in enumerate((velocity, epsilon, delta)):
        loads.append(pltpu.make_async_copy(array, raw_model.at[i], load_sems.at[i]))
    for i, array in enumerate((source, receiver)):
        loads.append(pltpu.make_async_copy(array, raw_fields.at[i], load_sems.at[3 + i]))
    for made in loads:
        made.start()

    barrier = pltpu.get_barrier_semaphore()
    greeted = all_peers() + [neighbour]
    for peer in greeted:
        pl.semaphore_signal(barrier, inc=1, device_id=peer, device_id_type=MESH)

    for made in loads[:3]:
        made.wait()
    picks = []
    for step in range(STEPS):
        for slot in range(2):
            hit = owner[step] == index * 2 + slot
            picks.append(jnp.full((8, LANES), jnp.where(hit, 1.0, 0.0), F32))

    def candidate(t, _):
        for k in range(8):
            place = (pl.ds(pl.multiple_of(t * 8, 8), 8), pl.ds(k * LANES, LANES))
            forms = []
            for slot in range(2):
                v = raw_model[(0, slot) + place]
                e = raw_model[(1, slot) + place]
                d = raw_model[(2, slot) + place]
                wide = 1.0 + 2.0 * d
                both = 1.0 / (v * wide)
                slowness = both * wide
                stretch = both * v
                curve = 5.0 * slowness * stretch
                forms.append((10.0 * slowness, curve, curve * ((e - d) * stretch * 0.125)))
            for step in range(STEPS):
                for n in range(3):
                    value = picks[step * 2] * forms[0][n] + picks[step * 2 + 1] * forms[1][n]
                    cand[at((step * 3 + n) * 64 + t * 8 + k)] = value
        return 0

    lax.fori_loop(0, 8, candidate, 0)
    pl.semaphore_wait(barrier, len(greeted))

    a_bufs, b_bufs, i_bufs = stream_bufs[0:6], stream_bufs[6:12], stream_bufs[12:18]
    a = Stream(cand, planes, 0, 256, ("xy", "z"), a_bufs, a_sends, a_recvs)
    b = Stream(cand, planes, 256, 128, ("z", "xy"), b_bufs, b_sends, b_recvs)
    for s in (a, b):
        s.core_out()

    for made in loads[3:]:
        made.wait()
    zero = jnp.zeros((8, LANES), F32)
    for field in (field0, field1):
        for i in range(HMAX * 4):
            field[at(67 * 4 * tile + i)] = zero
    delay = jnp.full((8, LANES), omega * 0.05, F32)
    pulse = (16.0 * jnp.cos(delay), -16.0 * jnp.sin(delay))

    def arrange(t, _):
        for c in range(4):
            for k in range(8):
                place = (pl.ds(pl.multiple_of(t * 8, 8), 8), pl.ds(k * LANES, LANES))
                value = raw_fields[(c // 2, c % 2, 0) + place]
                if c < 2:
                    row = lax.broadcasted_iota(jnp.int32, (8, LANES), 0) + (tile * ROWS + t * 8)
                    col = lax.broadcasted_iota(jnp.int32, (8, LANES), 1) + k * LANES
                    for s in range(4):
                        hit = (row == srows[s]) & (col == scols[s])
                        value = value + jnp.where(hit, pulse[c], 0.0)
                field0[pl.ds((t * 8 + HMAX) * 32 + c * 8 + k, 8, stride=32)] = value
        return 0

    def weights():
        for step in range(STEPS):
            live = [jnp.where(reach[step] >= n, t, 0.0) for n, t in zip(NEEDED, TAPERS)]
            total = live[0] * COUNTS[0]
            for n, w in zip(COUNTS[1:], live[1:]):
                total = total + w * n
            inverse = 1.0 / jnp.full((8, LANES), total, F32)
            for i, w in enumerate(live):
                coef[at(step * 10 + i)] = inverse * w

    def halo(field, slot):
        made = pltpu.make_async_remote_copy(
            src_ref=field.at[at((64 - 61 * tile) * 4, HMAX * 4)],
            dst_ref=field.at[at(67 * tile * 4, HMAX * 4)],
            send_sem=halo_sends.at[slot],
            recv_sem=halo_recvs.at[slot],
            device_id=neighbour,
            device_id_type=MESH,
        )
        made.start()
        return made

    for s in (a, b):
        s.land()
        s.core_sum()
        s.scatter1()
    lax.fori_loop(0, 8, arrange, 0)
    halo0 = halo(field0, 0)
    for s in (a, b):
        s.land()
        s.sum1_()
        s.scatter2()
    weights()
    lax.fori_loop(HMAX, HMAX + ROWS, spread(field0, pairs), 0)
    for s in (a, b):
        s.land()
        s.sum2_()
        s.gather2()
    halo0.wait()
    lax.fori_loop(0, HMAX, spread(field0, pairs), 0)
    lax.fori_loop(HMAX + ROWS, TALL, spread(field0, pairs), 0)
    for s in (a, b):
        s.land()
        s.gather1()
    for s in (a, b):
        s.land()
        s.core_back()
    for s in (a, b):
        s.land()

    def row_at(i):
        return (1 - tile) * (ROWS - 1) + (2 * tile - 1) * i

    def first_step(i, _):
        x = row_at(i)
        out = one_row(field0, pairs, planes, coef, 0, x, omega)
        for c in range(4):
            field1[at((x + HMAX) * 4 + c)] = out[c]
        images[at(x)] = out[0] * out[2] + out[1] * out[3]
        return 0

    lax.fori_loop(0, HMAX, first_step, 0)
    halo1 = halo(field1, 1)
    lax.fori_loop(HMAX, ROWS, first_step, 0)

    lax.fori_loop(HMAX, HMAX + ROWS, spread(field1, pairs), 0)
    halo1.wait()
    lax.fori_loop(0, HMAX, spread(field1, pairs), 0)
    lax.fori_loop(HMAX + ROWS, TALL, spread(field1, pairs), 0)

    def second_step(x, _):
        out = one_row(field1, pairs, planes, coef, 1, x, omega)
        for c in range(4):
            field2[at(x * 4 + c)] = out[c]
        images[at(ROWS + x)] = out[0] * out[2] + out[1] * out[3]
        return 0

    lax.fori_loop(0, ROWS, second_step, 0)

    i = Stream(images, image_sum, 0, IMAGE_UNITS, ("xy", "z"), i_bufs, i_sends, i_recvs)
    i.core_out()

    def restore(t, _):
        for c in range(4):
            for k in range(8):
                place = (pl.ds(pl.multiple_of(t * 8, 8), 8), pl.ds(k * LANES, LANES))
                raw_fields[(c // 2, c % 2, 0) + place] = field2[
                    pl.ds(t * 256 + c * 8 + k, 8, stride=32)
                ]
        return 0

    i.land()
    i.core_sum()
    i.scatter1()
    lax.fori_loop(0, 8, restore, 0)
    stores = [
        pltpu.make_async_copy(raw_fields.at[0], source_out, load_sems.at[3]),
        pltpu.make_async_copy(raw_fields.at[1], receiver_out, load_sems.at[4]),
    ]
    for made in stores:
        made.start()
    i.land()
    i.sum1_()
    i.scatter2()
    i.land()
    i.sum2_()
    i.gather2()
    i.land()
    i.gather1()
    i.land()
    i.core_back()
    i.land()

    def picture(t, _):
        for step in range(STEPS):
            for k in range(8):
                place = (pl.ds(pl.multiple_of(t * 8, 8), 8), pl.ds(k * LANES, LANES))
                value = image_sum[pl.ds(step * 512 + t * 64 + k, 8, stride=8)]
                image_nat[(step,) + place] = value * GAIN
        return 0

    lax.fori_loop(0, 8, picture, 0)
    last = pltpu.make_async_copy(image_nat, image_out, load_sems.at[0])
    last.start()
    for made in stores + [last]:
        made.wait()
    for s in (a, b, i):
        s.finish()


def per_device(*args):
    source, receiver, omegas, velocity, epsilon, delta, owner, reach, srows, scols = args
    smem = pl.BlockSpec(memory_space=pltpu.SMEM)
    hbm = pl.BlockSpec(memory_space=pl.ANY)

    def block(n):
        return pltpu.VMEM((n * 8, LANES), F32)

    sems = [pltpu.SemaphoreType.DMA((Stream.SEMS,))] * 6
    return pl.pallas_call(
        kernel,
        out_shape=(
            jax.ShapeDtypeStruct(source.shape, F32),
            jax.ShapeDtypeStruct(receiver.shape, F32),
            jax.ShapeDtypeStruct((STEPS, ROWS, 1024), F32),
        ),
        in_specs=[smem] * 5 + [hbm] * 5,
        out_specs=(hbm, hbm, hbm),
        scratch_shapes=[
            pltpu.VMEM((2, 2, 1, ROWS, 1024), F32),
            pltpu.VMEM((3, 2, ROWS, 1024), F32),
            block(PLANE_UNITS),
            block(PLANE_UNITS),
            block(TALL * 4),
            block(TALL * 4),
            block(ROWS * 4),
            block(TALL * 4),
            block(TALL * 4),
            block(TALL * 4),
            block(20),
            block(IMAGE_UNITS),
            block(IMAGE_UNITS),
            pltpu.VMEM((STEPS, ROWS, 1024), F32),
            pltpu.SemaphoreType.DMA((5,)),
            pltpu.SemaphoreType.DMA((2,)),
            pltpu.SemaphoreType.DMA((2,)),
        ]
        + sems
        + Stream.scratch(256)
        + Stream.scratch(128)
        + Stream.scratch(IMAGE_UNITS),
        compiler_params=pltpu.CompilerParams(
            collective_id=0, has_side_effects=True, vmem_limit_bytes=48 << 20
        ),
        name="migrate",
    )(omegas, owner, reach, srows, scols, source, receiver, velocity, epsilon, delta)


def solution(mesh):
    in_specs = (
        P(None, "freq", "tile", None),
        P(None, "freq", "tile", None),
        P("freq"),
        P("freq", "tile", None),
        P("freq", "tile", None),
        P("freq", "tile", None),
        P(),
        P(),
        P(),
        P(),
    )
    out_specs = (
        P(None, "freq", "tile", None),
        P(None, "freq", "tile", None),
        P(None, "tile", None),
    )
    return jax.shard_map(
        per_device, mesh=mesh, in_specs=in_specs, out_specs=out_specs, check_vma=False
    )
```

time: 2190 us -> 94.8 us (0.04)
  waiting for transfers between devices: 2030 us -> 0 us
  other arithmetic: 110 us -> 0 us
  Pallas kernels: 0 us -> 84.2 us
    psum x2 -> x0, waiting for transfers between devices: 2030 us -> none  [the longest x1 1030 us: broadcast(): return lax.psum(block, axis)]
    pallas_call x0 -> x1, Pallas kernels: none -> 84.2 us  [per_device(): pl.pallas_call(kernel, out_shape=(jax.ShapeDtypeStruct(source.shape, F32)...]
    another operation x25 -> x0, other arithmetic: 73.2 us -> none  [the longest x23 71.7 us: extrapolate(): jnp.stack([weight_real * gathered[0] - weight_imag * gathered[1], weight_...]
    add x10 -> x0, other arithmetic: 26.5 us -> none  [the longest x7 23.8 us: extrapolate(): gathered = piece if gathered is None else gathered + piece]
  transfers between devices with their start and end apart: 6 -> 0, of which waited for: 3 -> 0; matrix products, arithmetic and copies ran while one was open for 1% -> 0% of each run, Pallas kernels for 0% -> 0%
where the time goes in v1:
time: 94.8 us; the launch traced here: 94.5 us
  Pallas kernels  84.2 us (89%)
  local copies, waits for them, and re-layouts  8.9 us (9%)
  between operations  1.35 us (1%)
    pallas_call x1, Pallas kernels, per_device(): pl.pallas_call(kernel, out_shape=(jax.ShapeDtypeStruct(source.shape, F32)...  84.2 us
    unnamed x21, local copies, waits for them, and re-layouts  8.9 us

profile of v1, /device:TPU:1, one launch (start us, length us, event | category | flops | bytes accessed | tf_op | source)
XLA Modules:
  0.0 94.5 jit_solution(8578677880360054912)
XLA Ops:
  0.6 0.0 copy-start.6
  0.6 0.0 copy-start.5
  1.3 0.0 copy-done.6
  1.3 0.0 copy-done.5
  1.3 0.0 copy-start
  1.3 1.0 %copy-done = f32[2,1,64,1024]{3,2,1,0:T(8,128)S(1)} copy-done((f32[2,1,64,1024]{3,2,1,0:T(8,128)S(1)}, f32[2,1,64,1024]{3,2,1,0:T(8,128)}, u32[]{:S(2)}) %copy-start) | copy-done | bytes 524312
  2.4 0.0 copy-start.1
  2.4 1.0 %copy-done.1 = f32[2,1,64,1024]{3,2,1,0:T(8,128)S(1)} copy-done((f32[2,1,64,1024]{3,2,1,0:T(8,128)S(1)}, f32[2,1,64,1024]{3,2,1,0:T(8,128)}, u32[]{:S(2)}) %copy-start.1) | copy-done | bytes 524312
  3.4 0.0 copy-start.2
  3.4 1.0 %copy-done.2 = f32[2,64,1024]{2,1,0:T(8,128)S(1)} copy-done((f32[2,64,1024]{2,1,0:T(8,128)S(1)}, f32[2,64,1024]{2,1,0:T(8,128)}, u32[]{:S(2)}) %copy-start.2) | copy-done | bytes 524312
  4.5 0.0 copy-start.3
  4.5 1.0 %copy-done.3 = f32[2,64,1024]{2,1,0:T(8,128)S(1)} copy-done((f32[2,64,1024]{2,1,0:T(8,128)S(1)}, f32[2,64,1024]{2,1,0:T(8,128)}, u32[]{:S(2)}) %copy-start.3) | copy-done | bytes 524312
  5.5 0.0 copy-start.4
  5.5 1.0 %copy-done.4 = f32[2,64,1024]{2,1,0:T(8,128)S(1)} copy-done((f32[2,64,1024]{2,1,0:T(8,128)S(1)}, f32[2,64,1024]{2,1,0:T(8,128)}, u32[]{:S(2)}) %copy-start.4) | copy-done | bytes 524312
  6.5 0.0 copy-start.7
  6.6 0.7 copy-done.7
  7.2 0.0 copy-start.8
  7.2 0.7 copy-done.8
  7.9 84.2 %migrate.1 = (f32[2,1,64,1024]{3,2,1,0:T(8,128)S(1)}, f32[2,1,64,1024]{3,2,1,0:T(8,128)S(1)}, f32[2,64,1024]{2,1,0:T(8,128)S(1)}) custom-call(f32[1]{0:T(128)S(6)} %copy.16.omegas, s32[256]{0:T(256)S(1)} %copy-done.5, s32[2]{0:T(128)S(1)} %copy-done.6, s32[4]{0:T(128)S(1)} %copy-done.7, s32[4]{0:T(128)S(1)} %copy-done.8, f32[2,1,64,1024]{3,2,1,0:T(8,128)S(1)} %copy-done, ...), custom_call_target="tpu_custom_call" | custom-call | tf_op jit(solution)/shard_map/migrate/pallas_call | solution.py:575
  92.1 0.8 copy.17
  92.9 0.8 copy.18
  93.7 0.8 copy.19
Async XLA Ops:
  0.6 0.7 copy-start.6
  0.6 0.7 copy-start.5
  1.3 1.0 %copy-start = (f32[2,1,64,1024]{3,2,1,0:T(8,128)S(1)}, f32[2,1,64,1024]{3,2,1,0:T(8,128)}, u32[]{:S(2)}) copy-start(f32[2,1,64,1024]{3,2,1,0:T(8,128)} %source.1) | copy-start | bytes 1572868
  2.4 1.0 %copy-start.1 = (f32[2,1,64,1024]{3,2,1,0:T(8,128)S(1)}, f32[2,1,64,1024]{3,2,1,0:T(8,128)}, u32[]{:S(2)}) copy-start(f32[2,1,64,1024]{3,2,1,0:T(8,128)} %receiver.1) | copy-start | bytes 1572868
  3.4 1.0 %copy-start.2 = (f32[2,64,1024]{2,1,0:T(8,128)S(1)}, f32[2,64,1024]{2,1,0:T(8,128)}, u32[]{:S(2)}) copy-start(f32[2,64,1024]{2,1,0:T(8,128)} %velocity.1) | copy-start | bytes 1572868
  4.5 1.0 %copy-start.3 = (f32[2,64,1024]{2,1,0:T(8,128)S(1)}, f32[2,64,1024]{2,1,0:T(8,128)}, u32[]{:S(2)}) copy-start(f32[2,64,1024]{2,1,0:T(8,128)} %epsilon.1) | copy-start | bytes 1572868
  5.5 1.0 %copy-start.4 = (f32[2,64,1024]{2,1,0:T(8,128)S(1)}, f32[2,64,1024]{2,1,0:T(8,128)}, u32[]{:S(2)}) copy-start(f32[2,64,1024]{2,1,0:T(8,128)} %delta.1) | copy-start | bytes 1572868
  6.5 0.7 copy-start.7
  7.2 0.7 copy-start.8

commit v2 on v1

--- a/solution.py
+++ b/solution.py
@@ -97,13 +97,22 @@
     return z, [(device((z + k) % 8, x, y, c), (z + k) % 8) for k in range(1, 8)]
 
 
+def flat_peers():
+    z, x, y, c = coords()
+    out = []
+    for k in range(1, 16):
+        px, py, pc = (x + k // 4) % 4, (y + k // 2 % 2) % 2, (c + k % 2) % 2
+        out.append((device(z, px, py, pc), px * 4 + py * 2 + pc))
+    return x * 4 + y * 2 + c, out
+
+
 def core_peer():
     z, x, y, c = coords()
     return device(z, x, y, 1 - c)
 
 
 def all_peers():
-    return [core_peer()] + [d for d, _ in xy_peers()[1]] + [d for d, _ in z_peers()[1]]
+    return [d for d, _ in flat_peers()[1]] + [d for d, _ in z_peers()[1]]
 
 
 class Stream:
@@ -233,44 +242,152 @@
             made.wait_send()
 
 
-def reduce_all(streams):
-    for s in streams:
-        s.core_out()
-    for s in streams:
-        s.land()
-        s.core_sum()
-        s.scatter1()
-    for s in streams:
-        s.land()
-        s.sum1_()
-        s.scatter2()
-    for s in streams:
-        s.land()
-        s.sum2_()
-        s.gather2()
-    for s in streams:
-        s.land()
-        s.gather1()
-    for s in streams:
-        s.land()
-        s.core_back()
-
-
-def spread(field, pairs):
+class Relay:
+    SEMS = 23
+
+    def __init__(self, src, res, base, units, bufs, sends, recvs):
+        self.src, self.res, self.base, self.units = src, res, base, units
+        self.core_in, self.half, self.shares, self.stack, self.total = bufs
+        self.sends, self.recvs = sends, recvs
+        self.z, self.ring = z_peers()
+        self.me, self.group = xy_peers()
+        self.core = coords()[3]
+        self.started = []
+
+    @staticmethod
+    def scratch(units):
+        def block(n):
+            return pltpu.VMEM((n * 8, LANES), F32)
+
+        share = units // 16
+        return [block(units // 2), block(units // 2), block(7 * share), block(8 * share), block(share)]
+
+    copy = Stream.copy
+    land = Stream.land
+    finish = Stream.finish
+    core_out = Stream.core_out
+    core_sum = Stream.core_sum
+
+    def scatter1(self):
+        n = self.units // 16
+        self.flying = [
+            self.copy(1 + k, self.half.at[at(j * n, n)], self.shares.at[at(k * n, n)], to)
+            for k, (to, j) in enumerate(self.ring)
+        ]
+
+    def exchange(self):
+        n = self.units // 16
+        total = self.half[at(self.z * n, n)]
+        for k in range(7):
+            total = total + self.shares[at(k * n, n)]
+        mine = at(self.me * n, n)
+        self.stack[mine] = total
+        self.flying = [
+            self.copy(8 + k, self.stack.at[mine], self.stack.at[mine], to)
+            for k, (to, j) in enumerate(self.group)
+        ]
+
+    def gather(self):
+        n = self.units // 16
+        place = self.base + self.core * (self.units // 2) + self.z * n
+        total = self.stack[at(0, n)]
+        for k in range(1, 8):
+            total = total + self.stack[at(k * n, n)]
+        self.total[...] = total
+        self.res[at(place, n)] = total
+        self.flying = [
+            self.copy(15 + k, self.total, self.res.at[at(place, n)], to)
+            for k, (to, j) in enumerate(self.ring)
+        ]
+
+    def core_back(self):
+        n = self.units // 2
+        mine = at(self.base + self.core * n, n)
+        self.flying = [self.copy(22, self.res.at[mine], self.res.at[mine], core_peer())]
+
+
+class Picture:
+    SEMS = 37
+    SHARE = ROWS // 16
+
+    def __init__(self, src, res, base, bufs, sends, recvs):
+        self.src, self.res, self.base = src, res, base
+        self.shares, self.stack, self.total = bufs
+        self.sends, self.recvs = sends, recvs
+        self.me, self.group = flat_peers()
+        self.z, self.ring = z_peers()
+        self.started = []
+
+    @staticmethod
+    def scratch():
+        n = Picture.SHARE * 8
+        return [
+            pltpu.VMEM((15 * n, LANES), F32),
+            pltpu.VMEM((8 * n, LANES), F32),
+            pltpu.VMEM((n, LANES), F32),
+        ]
+
+    copy = Stream.copy
+    land = Stream.land
+    finish = Stream.finish
+
+    def scatter(self):
+        n = self.SHARE
+        self.flying = [
+            self.copy(k, self.src.at[at(self.base + j * n, n)], self.shares.at[at(k * n, n)], to)
+            for k, (to, j) in enumerate(self.group)
+        ]
+
+    def exchange(self):
+        n = self.SHARE
+        for i in range(n):
+            total = self.src[at(self.base + self.me * n + i)]
+            for k in range(15):
+                total = total + self.shares[at(k * n + i)]
+            self.stack[at(self.z * n + i)] = total
+        mine = at(self.z * n, n)
+        self.flying = [
+            self.copy(15 + k, self.stack.at[mine], self.stack.at[mine], to)
+            for k, (to, j) in enumerate(self.ring)
+        ]
+
+    def gather(self):
+        n = self.SHARE
+        place = self.base + self.me * n
+        for i in range(n):
+            total = self.stack[at(i)]
+            for k in range(1, 8):
+                total = total + self.stack[at(k * n + i)]
+            total = total * GAIN
+            self.total[at(i)] = total
+            self.res[at(place + i)] = total
+        self.flying = [
+            self.copy(22 + k, self.total, self.res.at[at(place, n)], to)
+            for k, (to, j) in enumerate(self.group)
+        ]
+
+
+def spread(here):
+    lane = lax.broadcasted_iota(jnp.int32, (8, LANES), 1)
+    block = lax.broadcasted_iota(jnp.int32, (8, LANES), 0)
+    above = jnp.where(block < 7, pltpu.roll(here, 7, 0), 0.0)
+    below = jnp.where(block > 0, pltpu.roll(here, 1, 0), 0.0)
+    out = []
+    for b in range(1, 4):
+        plus = pltpu.roll(jnp.where(lane < b, above, here), LANES - b, 1)
+        minus = pltpu.roll(jnp.where(lane >= LANES - b, below, here), b, 1)
+        out.append(plus + minus)
+    return out
+
+
+def spread_rows(field, pairs, first, count):
     def body(i, _):
-        lane = lax.broadcasted_iota(jnp.int32, (8, LANES), 1)
-        block = lax.broadcasted_iota(jnp.int32, (8, LANES), 0)
         for c in range(4):
-            here = field[at(i * 4 + c)]
-            above = jnp.where(block < 7, pltpu.roll(here, 7, 0), 0.0)
-            below = jnp.where(block > 0, pltpu.roll(here, 1, 0), 0.0)
-            for b in range(1, 4):
-                plus = pltpu.roll(jnp.where(lane < b, above, here), LANES - b, 1)
-                minus = pltpu.roll(jnp.where(lane >= LANES - b, below, here), b, 1)
-                pairs[b - 1][at(i * 4 + c)] = plus + minus
+            for pair, value in zip(pairs, spread(field[c, at(first + i)])):
+                pair[c, at(first + i)] = value
         return 0
 
-    return body
+    lax.fori_loop(0, count, body, 0, unroll=4 if count % 4 == 0 else 1)
 
 
 def weights_of(planes, step, x, omega):
@@ -278,7 +395,8 @@
 
     def row(array):
         start = (step * 3 + array) * 512 + t * 64 + s
-        return planes[pl.ds(start, 8, stride=8)]
+        both = [planes[pl.ds(start + i, 8, stride=8)] for i in range(2)]
+        return jnp.concatenate(both, axis=0)
 
     turn = cis((0.5 * omega) * row(0))
     turn = square(turn)
@@ -307,7 +425,7 @@
     return turn, g
 
 
-def one_row(field, pairs, planes, coef, step, x, omega):
+def two_rows(field, pairs, planes, coef, step, x, omega):
     rows = [field] + list(pairs)
 
     def gathered(r, c):
@@ -317,17 +435,17 @@
                 if a * a + b * b != r:
                     continue
                 for shift in sorted({a, -a}):
-                    piece = rows[b][at((x + HMAX + shift) * 4 + c)]
+                    piece = rows[b][c, at(x + HMAX + shift, 2)]
                     total = piece if total is None else total + piece
         return total
 
     turn, g = weights_of(planes, step, x, omega)
-    first = coef[at(step * 10)]
+    first = coef[at(step * 20, 2)]
     acc = [first * gathered(0, c) for c in range(4)]
     for index, r in enumerate(GROUPS):
         if r == 0:
             continue
-        scale = coef[at(step * 10 + index)]
+        scale = coef[at(step * 20 + index * 2, 2)]
         wr, wi = g[r][0] * scale, g[r][1] * scale
         sr, si, rr, ri = [gathered(r, c) for c in range(4)]
         acc[0] = acc[0] + (wr * sr - wi * si)
@@ -348,23 +466,26 @@
 
 
 def kernel(
-    omegas, owner, reach, srows, scols, source, receiver, velocity, epsilon, delta,
+    omegas_in, owner_in, reach_in, srows_in, scols_in, source, receiver, velocity, epsilon, delta,
     source_out, receiver_out, image_out,
-    raw_fields, raw_model, cand, planes, field0, field1, field2, pair1, pair2, pair3, coef, images,
-    image_sum, image_nat, load_sems, halo_sends, halo_recvs, a_sends, a_recvs, b_sends, b_recvs,
-    i_sends, i_recvs, *stream_bufs,
+    omegas, owner, reach, srows, scols,
+    raw_fields, raw_model, cand, planes, field0, field1, field2, pair1, pair2, pair3, next1, next2,
+    next3, coef, images, image_sum, image_nat, load_sems, halo_sends, halo_recvs, *rest,
 ):
+    sems, bufs = rest[:12], rest[12:]
     tile = lax.axis_index("tile")
     index = lax.axis_index("freq")
     neighbour = {"tile": 1 - tile}
-    omega = omegas[0]
-    pairs = (pair1, pair2, pair3)
+    pairs, nexts = (pair1, pair2, pair3), (next1, next2, next3)
 
     loads = []
     for i, array in enumerate((velocity, epsilon, delta)):
         loads.append(pltpu.make_async_copy(array, raw_model.at[i], load_sems.at[i]))
     for i, array in enumerate((source, receiver)):
         loads.append(pltpu.make_async_copy(array, raw_fields.at[i], load_sems.at[3 + i]))
+    smalls = ((omegas_in, omegas), (owner_in, owner), (reach_in, reach), (srows_in, srows), (scols_in, scols))
+    for i, (array, place) in enumerate(smalls):
+        loads.append(pltpu.make_async_copy(array, place, load_sems.at[5 + i]))
     for made in loads:
         made.start()
 
@@ -373,8 +494,9 @@
     for peer in greeted:
         pl.semaphore_signal(barrier, inc=1, device_id=peer, device_id_type=MESH)
 
-    for made in loads[:3]:
+    for made in loads[:3] + loads[5:]:
         made.wait()
+    omega = omegas[0]
     picks = []
     for step in range(STEPS):
         for slot in range(2):
@@ -404,18 +526,22 @@
     lax.fori_loop(0, 8, candidate, 0)
     pl.semaphore_wait(barrier, len(greeted))
 
-    a_bufs, b_bufs, i_bufs = stream_bufs[0:6], stream_bufs[6:12], stream_bufs[12:18]
-    a = Stream(cand, planes, 0, 256, ("xy", "z"), a_bufs, a_sends, a_recvs)
-    b = Stream(cand, planes, 256, 128, ("z", "xy"), b_bufs, b_sends, b_recvs)
-    for s in (a, b):
+    a0 = Stream(cand, planes, 0, 128, ("xy", "z"), bufs[0:6], sems[0], sems[1])
+    a1 = Stream(cand, planes, 192, 128, ("xy", "z"), bufs[6:12], sems[2], sems[3])
+    b0 = Relay(cand, planes, 128, 64, bufs[12:17], sems[4], sems[5])
+    b1 = Relay(cand, planes, 320, 64, bufs[17:22], sems[6], sems[7])
+    p0 = Picture(images, image_sum, 0, bufs[22:25], sems[8], sems[9])
+    p1 = Picture(images, image_sum, ROWS, bufs[25:28], sems[10], sems[11])
+    for s in (a0, b0, a1, b1):
         s.core_out()
 
-    for made in loads[3:]:
+    for made in loads[3:5]:
         made.wait()
     zero = jnp.zeros((8, LANES), F32)
-    for field in (field0, field1):
-        for i in range(HMAX * 4):
-            field[at(67 * 4 * tile + i)] = zero
+    for field in (field0, field1) + pairs + nexts:
+        for i in range(HMAX):
+            for c in range(4):
+                field[c, at(67 * tile + i)] = zero
     delay = jnp.full((8, LANES), omega * 0.05, F32)
     pulse = (16.0 * jnp.cos(delay), -16.0 * jnp.sin(delay))
 
@@ -430,7 +556,7 @@
                     for s in range(4):
                         hit = (row == srows[s]) & (col == scols[s])
                         value = value + jnp.where(hit, pulse[c], 0.0)
-                field0[pl.ds((t * 8 + HMAX) * 32 + c * 8 + k, 8, stride=32)] = value
+                field0[c, pl.ds((t * 8 + HMAX) * 8 + k, 8, stride=8)] = value
         return 0
 
     def weights():
@@ -441,12 +567,13 @@
                 total = total + w * n
             inverse = 1.0 / jnp.full((8, LANES), total, F32)
             for i, w in enumerate(live):
-                coef[at(step * 10 + i)] = inverse * w
+                coef[at(step * 20 + i * 2)] = inverse * w
+                coef[at(step * 20 + i * 2 + 1)] = inverse * w
 
     def halo(field, slot):
         made = pltpu.make_async_remote_copy(
-            src_ref=field.at[at((64 - 61 * tile) * 4, HMAX * 4)],
-            dst_ref=field.at[at(67 * tile * 4, HMAX * 4)],
+            src_ref=field.at[:, at(64 - 61 * tile, HMAX)],
+            dst_ref=field.at[:, at(67 * tile, HMAX)],
             send_sem=halo_sends.at[slot],
             recv_sem=halo_recvs.at[slot],
             device_id=neighbour,
@@ -455,78 +582,99 @@
         made.start()
         return made
 
-    for s in (a, b):
+    for s in (a0, b0):
         s.land()
         s.core_sum()
         s.scatter1()
     lax.fori_loop(0, 8, arrange, 0)
     halo0 = halo(field0, 0)
-    for s in (a, b):
+    a0.land()
+    a0.sum1_()
+    a0.scatter2()
+    b0.land()
+    b0.exchange()
+    for s in (a1, b1):
         s.land()
-        s.sum1_()
-        s.scatter2()
+        s.core_sum()
+        s.scatter1()
     weights()
-    lax.fori_loop(HMAX, HMAX + ROWS, spread(field0, pairs), 0)
-    for s in (a, b):
-        s.land()
-        s.sum2_()
-        s.gather2()
+    spread_rows(field0, pairs, HMAX, ROWS)
     halo0.wait()
-    lax.fori_loop(0, HMAX, spread(field0, pairs), 0)
-    lax.fori_loop(HMAX + ROWS, TALL, spread(field0, pairs), 0)
-    for s in (a, b):
-        s.land()
-        s.gather1()
-    for s in (a, b):
-        s.land()
-        s.core_back()
-    for s in (a, b):
-        s.land()
-
-    def row_at(i):
-        return (1 - tile) * (ROWS - 1) + (2 * tile - 1) * i
+    spread_rows(field0, pairs, 67 * (1 - tile), HMAX)
+    a0.land()
+    a0.sum2_()
+    a0.gather2()
+    b0.land()
+    b0.gather()
+    a1.land()
+    a1.sum1_()
+    a1.scatter2()
+    b1.land()
+    b1.exchange()
+    a0.land()
+    a0.gather1()
+    b0.land()
+    b0.core_back()
+    a1.land()
+    a1.sum2_()
+    a1.gather2()
+    b1.land()
+    b1.gather()
+    a0.land()
+    a0.core_back()
+    b0.land()
+    a0.land()
+    a1.land()
+    a1.gather1()
+    b1.land()
+    b1.core_back()
 
     def first_step(i, _):
-        x = row_at(i)
-        out = one_row(field0, pairs, planes, coef, 0, x, omega)
+        x = (1 - tile) * (ROWS - 2) + (2 * tile - 1) * (i * 2)
+        out = two_rows(field0, pairs, planes, coef, 0, x, omega)
         for c in range(4):
-            field1[at((x + HMAX) * 4 + c)] = out[c]
-        images[at(x)] = out[0] * out[2] + out[1] * out[3]
+            field1[c, at(x + HMAX, 2)] = out[c]
+            for h in range(2):
+                for pair, value in zip(nexts, spread(out[c][h * 8 : h * 8 + 8])):
+                    pair[c, at(x + HMAX + h)] = value
+        images[at(x, 2)] = out[0] * out[2] + out[1] * out[3]
         return 0
 
-    lax.fori_loop(0, HMAX, first_step, 0)
+    lax.fori_loop(0, 2, first_step, 0)
     halo1 = halo(field1, 1)
-    lax.fori_loop(HMAX, ROWS, first_step, 0)
-
-    lax.fori_loop(HMAX, HMAX + ROWS, spread(field1, pairs), 0)
+    lax.fori_loop(2, 20, first_step, 0)
+    a1.land()
+    a1.core_back()
+    lax.fori_loop(20, ROWS // 2, first_step, 0)
+    p0.scatter()
     halo1.wait()
-    lax.fori_loop(0, HMAX, spread(field1, pairs), 0)
-    lax.fori_loop(HMAX + ROWS, TALL, spread(field1, pairs), 0)
-
-    def second_step(x, _):
-        out = one_row(field1, pairs, planes, coef, 1, x, omega)
+    spread_rows(field1, nexts, 67 * (1 - tile), HMAX)
+    a1.land()
+    b1.land()
+
+    def second_step(i, _):
+        x = i * 2
+        out = two_rows(field1, nexts, planes, coef, 1, x, omega)
         for c in range(4):
-            field2[at(x * 4 + c)] = out[c]
-        images[at(ROWS + x)] = out[0] * out[2] + out[1] * out[3]
+            field2[c, at(x, 2)] = out[c]
+        images[at(ROWS + x, 2)] = out[0] * out[2] + out[1] * out[3]
         return 0
 
-    lax.fori_loop(0, ROWS, second_step, 0)
-
-    i = Stream(images, image_sum, 0, IMAGE_UNITS, ("xy", "z"), i_bufs, i_sends, i_recvs)
-    i.core_out()
+    lax.fori_loop(0, 28, second_step, 0)
+    p0.land()
+    p0.exchange()
+    lax.fori_loop(28, ROWS // 2, second_step, 0)
+    p1.scatter()
 
     def restore(t, _):
         for c in range(4):
             for k in range(8):
                 place = (pl.ds(pl.multiple_of(t * 8, 8), 8), pl.ds(k * LANES, LANES))
                 raw_fields[(c // 2, c % 2, 0) + place] = field2[
-                    pl.ds(t * 256 + c * 8 + k, 8, stride=32)
+                    c, pl.ds(t * 64 + k, 8, stride=8)
                 ]
         return 0
 
-    i.land()
-    i.core_sum()
-    i.scatter1()
     lax.fori_loop(0, 8, restore, 0)
     stores = [
         pltpu.make_async_copy(raw_fields.at[0], source_out, load_sems.at[3]),
@@ -534,24 +682,21 @@
     ]
     for made in stores:
         made.start()
-    i.land()
-    i.sum1_()
-    i.scatter2()
-    i.land()
-    i.sum2_()
-    i.gather2()
-    i.land()
-    i.gather1()
-    i.land()
-    i.core_back()
-    i.land()
+    p0.land()
+    p0.gather()
+    p1.land()
+    p1.exchange()
+    p1.land()
+    p1.gather()
+    p0.land()
+    p1.land()
 
     def picture(t, _):
         for step in range(STEPS):
             for k in range(8):
                 place = (pl.ds(pl.multiple_of(t * 8, 8), 8), pl.ds(k * LANES, LANES))
                 value = image_sum[pl.ds(step * 512 + t * 64 + k, 8, stride=8)]
-                image_nat[(step,) + place] = value * GAIN
+                image_nat[(step,) + place] = value
         return 0
 
     lax.fori_loop(0, 8, picture, 0)
@@ -559,56 +704,86 @@
     last.start()
     for made in stores + [last]:
         made.wait()
-    for s in (a, b, i):
+    for s in (a0, b0, a1, b1, p0, p1):
         s.finish()
+
+
+def hand_over(*refs):
+    between, sems = refs[6:9], refs[9]
+    loads = [pltpu.make_async_copy(refs[i], between[i], sems.at[i]) for i in range(3)]
+    stores = [pltpu.make_async_copy(between[i], refs[3 + i], sems.at[3 + i]) for i in range(3)]
+    for made in loads:
+        made.start()
+    for load, store in zip(loads, stores):
+        load.wait()
+        store.start()
+    for made in stores:
+        made.wait()
 
 
 def per_device(*args):
     source, receiver, omegas, velocity, epsilon, delta, owner, reach, srows, scols = args
-    smem = pl.BlockSpec(memory_space=pltpu.SMEM)
     hbm = pl.BlockSpec(memory_space=pl.ANY)
+    out_shape = (
+        jax.ShapeDtypeStruct(source.shape, F32),
+        jax.ShapeDtypeStruct(receiver.shape, F32),
+        jax.ShapeDtypeStruct((STEPS, ROWS, 1024), F32),
+    )
 
     def block(n):
         return pltpu.VMEM((n * 8, LANES), F32)
 
-    sems = [pltpu.SemaphoreType.DMA((Stream.SEMS,))] * 6
-    return pl.pallas_call(
+    def plane(n):
+        return pltpu.VMEM((4, n * 8, LANES), F32)
+
+    def small(array):
+        return pltpu.SMEM(array.shape, array.dtype)
+
+    counts = [Stream.SEMS] * 4 + [Relay.SEMS] * 4 + [Picture.SEMS] * 4
+    made = pl.pallas_call(
         kernel,
-        out_shape=(
-            jax.ShapeDtypeStruct(source.shape, F32),
-            jax.ShapeDtypeStruct(receiver.shape, F32),
-            jax.ShapeDtypeStruct((STEPS, ROWS, 1024), F32),
-        ),
-        in_specs=[smem] * 5 + [hbm] * 5,
+        out_shape=out_shape,
+        in_specs=[hbm] * 10,
         out_specs=(hbm, hbm, hbm),
-        scratch_shapes=[
+        scratch_shapes=[small(array) for array in (omegas, owner, reach, srows, scols)]
+        + [
             pltpu.VMEM((2, 2, 1, ROWS, 1024), F32),
             pltpu.VMEM((3, 2, ROWS, 1024), F32),
             block(PLANE_UNITS),
             block(PLANE_UNITS),
-            block(TALL * 4),
-            block(TALL * 4),
-            block(ROWS * 4),
-            block(TALL * 4),
-            block(TALL * 4),
-            block(TALL * 4),
-            block(20),
+            plane(TALL),
+            plane(TALL),
+            plane(ROWS),
+        ]
+        + [plane(TALL)] * 6
+        + [
+            block(40),
             block(IMAGE_UNITS),
             block(IMAGE_UNITS),
             pltpu.VMEM((STEPS, ROWS, 1024), F32),
-            pltpu.SemaphoreType.DMA((5,)),
+            pltpu.SemaphoreType.DMA((10,)),
             pltpu.SemaphoreType.DMA((2,)),
             pltpu.SemaphoreType.DMA((2,)),
         ]
-        + sems
-        + Stream.scratch(256)
-        + Stream.scratch(128)
-        + Stream.scratch(IMAGE_UNITS),
+        + [pltpu.SemaphoreType.DMA((n,)) for n in counts]
+        + Stream.scratch(128) * 2
+        + Relay.scratch(64) * 2
+        + Picture.scratch() * 2,
         compiler_params=pltpu.CompilerParams(
-            collective_id=0, has_side_effects=True, vmem_limit_bytes=48 << 20
+            collective_id=0, has_side_effects=True, vmem_limit_bytes=52 << 20
         ),
         name="migrate",
     )(omegas, owner, reach, srows, scols, source, receiver, velocity, epsilon, delta)
+    return pl.pallas_call(
+        hand_over,
+        out_shape=out_shape,
+        in_specs=[hbm] * 3,
+        out_specs=(hbm, hbm, hbm),
+        scratch_shapes=[pltpu.VMEM(o.shape, F32) for o in out_shape]
+        + [pltpu.SemaphoreType.DMA((6,))],
+        compiler_params=pltpu.CompilerParams(vmem_limit_bytes=52 << 20),
+        name="hand_over",
+    )(*made)
 
 
 def solution(mesh):

time: 94.8 us -> 73.8 us (0.78)
  Pallas kernels: 84.2 us -> 71 us
  local copies, waits for them, and re-layouts: 8.9 us -> 1.31 us
    pallas_call x1 -> x2, Pallas kernels: 84.2 us -> 71 us  [the longest x1 69.7 us: per_device(): pl.pallas_call(kernel, out_shape=out_shape, in_specs=[hbm] * 10, out_spec...]
    unnamed x21 -> x8, local copies, waits for them, and re-layouts: 8.9 us -> 1.31 us
where the time goes in v2:
time: 73.8 us; the launch traced here: 73.6 us
  Pallas kernels  71 us (96%)
  between operations  1.35 us (2%)
  local copies, waits for them, and re-layouts  1.31 us (2%)
    pallas_call x1, Pallas kernels, per_device(): pl.pallas_call(kernel, out_shape=out_shape, in_specs=[hbm] * 10, out_spec...  69.7 us

profile of v2, /device:TPU:1, one launch (start us, length us, event | category | flops | bytes accessed | tf_op | source)
XLA Modules:
  0.0 73.6 jit_solution(930026563959617616)
XLA Ops:
  0.6 0.0 copy-start.1
  0.6 0.0 copy-start
  1.3 0.0 copy-done.1
  1.3 0.0 copy-done
  1.3 0.0 copy-start.2
  1.3 0.6 copy-done.2
  2.0 0.0 copy-start.3
  2.0 0.7 copy-done.3
  2.7 69.7 %migrate.1 = (f32[2,1,64,1024]{3,2,1,0:T(8,128)S(1)}, f32[2,1,64,1024]{3,2,1,0:T(8,128)S(1)}, f32[2,64,1024]{2,1,0:T(8,128)S(1)}) custom-call(f32[1]{0:T(128)S(6)} %copy.13.omegas_in, s32[256]{0:T(256)S(1)} %copy-done, s32[2]{0:T(128)S(1)} %copy-done.1, s32[4]{0:T(128)S(1)} %copy-done.2, s32[4]{0:T(128)S(1)} %copy-done.3, f32[2,1,64,1024]{3,2,1,0:T(8,128)} %source.1, ...), custom_call_target="tpu_custom_call" | custom-call | tf_op jit(solution)/shard_map/migrate/pallas_call | solution.py:743
  72.3 1.3 %hand_over.1 = (f32[2,1,64,1024]{3,2,1,0:T(8,128)}, f32[2,1,64,1024]{3,2,1,0:T(8,128)}, f32[2,64,1024]{2,1,0:T(8,128)}) custom-call(f32[2,1,64,1024]{3,2,1,0:T(8,128)S(1)} %get-tuple-element.6.refs_0_, f32[2,1,64,1024]{3,2,1,0:T(8,128)S(1)} %get-tuple-element.7.refs_1_, f32[2,64,1024]{2,1,0:T(8,128)S(1)} %get-tuple-element.8.refs_2_), custom_call_target="tpu_custom_call" | custom-call | tf_op jit(solution)/shard_map/hand_over/pallas_call | solution.py:777
Async XLA Ops:
  0.6 0.7 copy-start.1
  0.6 0.7 copy-start
  1.3 0.7 copy-start.2
  2.0 0.7 copy-start.3

commit v3 on v2

--- a/solution.py
+++ b/solution.py
@@ -86,7 +86,7 @@
 def xy_peers():
     z, x, y, c = coords()
     out = []
-    for k in range(1, 8):
+    for k in (5, 4, 3, 7, 2, 6, 1):
         px, py = (x + k // 2) % 4, (y + k % 2) % 2
         out.append((device(z, px, py, c), px * 2 + py))
     return x * 2 + y, out
@@ -94,13 +94,13 @@
 
 def z_peers():
     z, x, y, c = coords()
-    return z, [(device((z + k) % 8, x, y, c), (z + k) % 8) for k in range(1, 8)]
+    return z, [(device((z + k) % 8, x, y, c), (z + k) % 8) for k in (4, 3, 5, 2, 6, 1, 7)]
 
 
 def flat_peers():
     z, x, y, c = coords()
     out = []
-    for k in range(1, 16):
+    for k in (10, 11, 8, 9, 6, 7, 14, 15, 4, 5, 12, 13, 2, 3, 1):
         px, py, pc = (x + k // 4) % 4, (y + k // 2 % 2) % 2, (c + k % 2) % 2
         out.append((device(z, px, py, pc), px * 4 + py * 2 + pc))
     return x * 4 + y * 2 + c, out
@@ -112,7 +112,7 @@
 
 
 def all_peers():
-    return [d for d, _ in flat_peers()[1]] + [d for d, _ in z_peers()[1]]
+    return [d for d, _ in z_peers()[1]] + [d for d, _ in flat_peers()[1]]
 
 
 class Stream:
@@ -240,6 +240,7 @@
     def finish(self):
         for made in self.started:
             made.wait_send()
+        self.started = []
 
 
 class Relay:
@@ -470,13 +471,18 @@
     source_out, receiver_out, image_out,
     omegas, owner, reach, srows, scols,
     raw_fields, raw_model, cand, planes, field0, field1, field2, pair1, pair2, pair3, next1, next2,
-    next3, coef, images, image_sum, image_nat, load_sems, halo_sends, halo_recvs, *rest,
+    next3, coef, images, image_sum, load_sems, halo_sends, halo_recvs, *rest,
 ):
     sems, bufs = rest[:12], rest[12:]
     tile = lax.axis_index("tile")
     index = lax.axis_index("freq")
     neighbour = {"tile": 1 - tile}
     pairs, nexts = (pair1, pair2, pair3), (next1, next2, next3)
+
+    barrier = pltpu.get_barrier_semaphore()
+    greeted = all_peers() + [neighbour]
+    for peer in greeted:
+        pl.semaphore_signal(barrier, inc=1, device_id=peer, device_id_type=MESH)
 
     loads = []
     for i, array in enumerate((velocity, epsilon, delta)):
@@ -488,11 +494,6 @@
         loads.append(pltpu.make_async_copy(array, place, load_sems.at[5 + i]))
     for made in loads:
         made.start()
-
-    barrier = pltpu.get_barrier_semaphore()
-    greeted = all_peers() + [neighbour]
-    for peer in greeted:
-        pl.semaphore_signal(barrier, inc=1, device_id=peer, device_id_type=MESH)
 
     for made in loads[:3] + loads[5:]:
         made.wait()
@@ -660,34 +661,32 @@
         images[at(ROWS + x, 2)] = out[0] * out[2] + out[1] * out[3]
         return 0
 
-    lax.fori_loop(0, 28, second_step, 0)
+    lax.fori_loop(0, ROWS // 2, second_step, 0)
+    p1.scatter()
     p0.land()
     p0.exchange()
-    lax.fori_loop(28, ROWS // 2, second_step, 0)
-    p1.scatter()
 
     def restore(t, _):
         for c in range(4):
             for k in range(8):
                 place = (pl.ds(pl.multiple_of(t * 8, 8), 8), pl.ds(k * LANES, LANES))
-                raw_fields[(c // 2, c % 2, 0) + place] = field2[
+                out = (source_out, receiver_out)[c // 2]
+                out[(c % 2, 0) + place] = field2[
                     c, pl.ds(t * 64 + k, 8, stride=8)
                 ]
         return 0
 
     lax.fori_loop(0, 8, restore, 0)
-    stores = [
-        pltpu.make_async_copy(raw_fields.at[0], source_out, load_sems.at[3]),
-        pltpu.make_async_copy(raw_fields.at[1], receiver_out, load_sems.at[4]),
-    ]
-    for made in stores:
-        made.start()
+    for s in (a0, b0, a1, b1):
+        s.finish()
     p0.land()
     p0.gather()
     p1.land()
     p1.exchange()
     p1.land()
     p1.gather()
+    for s in (p0, p1):
+        s.finish()
     p0.land()
     p1.land()
 
@@ -696,16 +695,10 @@
             for k in range(8):
                 place = (pl.ds(pl.multiple_of(t * 8, 8), 8), pl.ds(k * LANES, LANES))
                 value = image_sum[pl.ds(step * 512 + t * 64 + k, 8, stride=8)]
-                image_nat[(step,) + place] = value
+                image_out[(step,) + place] = value
         return 0
 
     lax.fori_loop(0, 8, picture, 0)
-    last = pltpu.make_async_copy(image_nat, image_out, load_sems.at[0])
-    last.start()
-    for made in stores + [last]:
-        made.wait()
-    for s in (a0, b0, a1, b1, p0, p1):
-        s.finish()
 
 
 def hand_over(*refs):
@@ -744,7 +737,7 @@
         kernel,
         out_shape=out_shape,
         in_specs=[hbm] * 10,
-        out_specs=(hbm, hbm, hbm),
+        out_specs=tuple([pl.BlockSpec(memory_space=pltpu.VMEM)] * 3),
         scratch_shapes=[small(array) for array in (omegas, owner, reach, srows, scols)]
         + [
             pltpu.VMEM((2, 2, 1, ROWS, 1024), F32),
@@ -760,7 +753,6 @@
             block(40),
             block(IMAGE_UNITS),
             block(IMAGE_UNITS),
-            pltpu.VMEM((STEPS, ROWS, 1024), F32),
             pltpu.SemaphoreType.DMA((10,)),
             pltpu.SemaphoreType.DMA((2,)),
             pltpu.SemaphoreType.DMA((2,)),

time: 73.8 us -> 67.8 us (0.919)
  Pallas kernels: 71 us -> 65 us
    pallas_call x1, Pallas kernels: 69.7 us -> 63.7 us  [per_device(): pl.pallas_call(kernel, out_shape=out_shape, in_specs=[hbm] * 10, out_spec...]
where the time goes in v3:
time: 67.8 us; the launch traced here: 67.7 us
  Pallas kernels  65 us (96%)
  between operations  1.35 us (2%)
  local copies, waits for them, and re-layouts  1.31 us (2%)
    pallas_call x1, Pallas kernels, per_device(): pl.pallas_call(kernel, out_shape=out_shape, in_specs=[hbm] * 10, out_spec...  63.7 us

profile of v3, /device:TPU:1, one launch (start us, length us, event | category | flops | bytes accessed | tf_op | source)
XLA Modules:
  0.0 67.7 jit_solution(8396749368542677254)
XLA Ops:
  0.6 0.0 copy-start.1
  0.6 0.0 copy-start
  1.3 0.0 copy-done.1
  1.3 0.0 copy-done
  1.3 0.0 copy-start.2
  1.3 0.6 copy-done.2
  2.0 0.0 copy-start.3
  2.0 0.7 copy-done.3
  2.7 63.7 %migrate.1 = (f32[2,1,64,1024]{3,2,1,0:T(8,128)S(1)}, f32[2,1,64,1024]{3,2,1,0:T(8,128)S(1)}, f32[2,64,1024]{2,1,0:T(8,128)S(1)}) custom-call(f32[1]{0:T(128)S(6)} %copy.13.omegas_in, s32[256]{0:T(256)S(1)} %copy-done, s32[2]{0:T(128)S(1)} %copy-done.1, s32[4]{0:T(128)S(1)} %copy-done.2, s32[4]{0:T(128)S(1)} %copy-done.3, f32[2,1,64,1024]{3,2,1,0:T(8,128)} %source.1, ...), custom_call_target="tpu_custom_call" | custom-call | tf_op jit(solution)/shard_map/migrate/pallas_call | solution.py:736
  66.4 1.3 %hand_over.1 = (f32[2,1,64,1024]{3,2,1,0:T(8,128)}, f32[2,1,64,1024]{3,2,1,0:T(8,128)}, f32[2,64,1024]{2,1,0:T(8,128)}) custom-call(f32[2,1,64,1024]{3,2,1,0:T(8,128)S(1)} %get-tuple-element.6.refs_0_, f32[2,1,64,1024]{3,2,1,0:T(8,128)S(1)} %get-tuple-element.7.refs_1_, f32[2,64,1024]{2,1,0:T(8,128)S(1)} %get-tuple-element.8.refs_2_), custom_call_target="tpu_custom_call" | custom-call | tf_op jit(solution)/shard_map/hand_over/pallas_call | solution.py:769
Async XLA Ops:
  0.6 0.7 %copy-start.1 = (s32[2]{0:T(128)S(1)}, s32[2]{0:T(128)}, u32[]{:S(2)}) copy-start(s32[2]{0:T(128)} %reach_in.1) | copy-start | bytes 28
  0.6 0.7 %copy-start = (s32[256]{0:T(256)S(1)}, s32[256]{0:T(256)}, u32[]{:S(2)}) copy-start(s32[256]{0:T(256)} %owner_in.1) | copy-start | bytes 3076
  1.3 0.7 copy-start.2
  2.0 0.7 copy-start.3

commit v4 on v3

--- a/solution.py
+++ b/solution.py
@@ -76,7 +76,7 @@
 
 def coords():
     f = lax.axis_index("freq")
-    return f // 16, (f // 4) % 4, (f // 2) % 2, f % 2
+    return lax.div(f, 16), lax.rem(lax.div(f, 4), 4), lax.rem(lax.div(f, 2), 2), lax.rem(f, 2)
 
 
 def device(z, x, y, c):
@@ -87,21 +87,21 @@
     z, x, y, c = coords()
     out = []
     for k in (5, 4, 3, 7, 2, 6, 1):
-        px, py = (x + k // 2) % 4, (y + k % 2) % 2
+        px, py = lax.rem(x + k // 2, 4), lax.rem(y + k % 2, 2)
         out.append((device(z, px, py, c), px * 2 + py))
     return x * 2 + y, out
 
 
 def z_peers():
     z, x, y, c = coords()
-    return z, [(device((z + k) % 8, x, y, c), (z + k) % 8) for k in (4, 3, 5, 2, 6, 1, 7)]
+    return z, [(device(lax.rem(z + k, 8), x, y, c), lax.rem(z + k, 8)) for k in (4, 3, 5, 2, 6, 1, 7)]
 
 
 def flat_peers():
     z, x, y, c = coords()
     out = []
     for k in (10, 11, 8, 9, 6, 7, 14, 15, 4, 5, 12, 13, 2, 3, 1):
-        px, py, pc = (x + k // 4) % 4, (y + k // 2 % 2) % 2, (c + k % 2) % 2
+        px, py, pc = lax.rem(x + k // 4, 4), lax.rem(y + k // 2 % 2, 2), lax.rem(c + k % 2, 2)
         out.append((device(z, px, py, pc), px * 4 + py * 2 + pc))
     return x * 4 + y * 2 + c, out
 
@@ -116,7 +116,7 @@
 
 
 class Stream:
-    SEMS = 30
+    SEMS = 6
 
     def __init__(self, src, res, base, units, order, bufs, sends, recvs):
         self.src, self.res, self.base, self.units = src, res, base, units
@@ -124,7 +124,7 @@
         self.sends, self.recvs = sends, recvs
         self.groups = [xy_peers() if o == "xy" else z_peers() for o in order]
         self.core = coords()[3]
-        self.started = []
+        self.done = 0
 
     @staticmethod
     def scratch(units):
@@ -140,64 +140,65 @@
             block(units // 16),
         ]
 
-    def copy(self, slot, src, dst, to):
-        made = pltpu.make_async_remote_copy(
-            src_ref=src,
-            dst_ref=dst,
-            send_sem=self.sends.at[slot],
-            recv_sem=self.recvs.at[slot],
-            device_id=to,
-            device_id_type=MESH,
-        )
-        made.start()
-        self.started.append(made)
-        return made
+    def send(self, phase, parts):
+        for src, dst, to in parts:
+            pltpu.make_async_remote_copy(
+                src_ref=src,
+                dst_ref=dst,
+                send_sem=self.sends.at[phase],
+                recv_sem=self.recvs.at[phase],
+                device_id=to,
+                device_id_type=MESH,
+            ).start()
+        self.phase = phase
+
+    def land(self):
+        whole = self.whole(self.phase)
+        pltpu.make_async_copy(whole, whole, self.recvs.at[self.phase]).wait()
+
+    def finish(self):
+        for phase in range(self.done, self.phase + 1):
+            whole = self.whole(phase)
+            pltpu.make_async_copy(whole, whole, self.sends.at[phase]).wait()
+        self.done = self.phase + 1
 
     def core_out(self):
         n = self.units // 2
         other = self.base + (1 - self.core) * n
-        self.flying = [self.copy(0, self.src.at[at(other, n)], self.core_in, core_peer())]
-
-    def land(self):
-        for made in self.flying:
-            made.wait_recv()
+        self.send(0, [(self.src.at[at(other, n)], self.core_in, core_peer())])
 
     def core_sum(self):
         n = self.units // 2
         mine = self.base + self.core * n
 
         def body(i, _):
-            self.half[at(i * 4, 4)] = self.src[at(mine + i * 4, 4)] + self.core_in[at(i * 4, 4)]
+            self.half[at(i * 16, 16)] = self.src[at(mine + i * 16, 16)] + self.core_in[at(i * 16, 16)]
             return 0
 
-        lax.fori_loop(0, n // 4, body, 0)
+        lax.fori_loop(0, n // 16, body, 0)
 
     def scatter1(self):
         n = self.units // 16
-        self.flying = [
-            self.copy(1 + k, self.half.at[at(j * n, n)], self.in1.at[at(k * n, n)], to)
+        self.send(1, [
+            (self.half.at[at(j * n, n)], self.in1.at[at(k * n, n)], to)
             for k, (to, j) in enumerate(self.groups[0][1])
-        ]
+        ])
 
     def sum1_(self):
         n = self.units // 16
         me = self.groups[0][0]
 
-        def body(i, _):
-            total = self.half[at(me * n + i)]
-            for k in range(7):
-                total = total + self.in1[at(k * n + i)]
-            self.sum1[at(i)] = total
-            return 0
-
-        lax.fori_loop(0, n, body, 0)
+        total = self.half[at(me * n, n)]
+        for k in range(7):
+            total = total + self.in1[at(k * n, n)]
+        self.sum1[...] = total
 
     def scatter2(self):
         n = self.units // 128
-        self.flying = [
-            self.copy(8 + k, self.sum1.at[at(j * n, n)], self.in2.at[at(k * n, n)], to)
+        self.send(2, [
+            (self.sum1.at[at(j * n, n)], self.in2.at[at(k * n, n)], to)
             for k, (to, j) in enumerate(self.groups[1][1])
-        ]
+        ])
 
     def sum2_(self):
         n = self.units // 128
@@ -211,40 +212,31 @@
     def gather2(self):
         n = self.units // 128
         me = self.groups[1][0]
-        self.flying = [
-            self.copy(15 + k, self.out1.at[at(me * n, n)], self.out1.at[at(me * n, n)], to)
-            for k, (to, j) in enumerate(self.groups[1][1])
-        ]
+        mine = at(me * n, n)
+        self.send(3, [(self.out1.at[mine], self.out1.at[mine], to) for to, j in self.groups[1][1]])
 
     def gather1(self):
         n = self.units // 16
         place = self.base + self.core * (self.units // 2) + self.groups[0][0] * n
-        self.flying = [
-            self.copy(22 + k, self.out1, self.res.at[at(place, n)], to)
-            for k, (to, j) in enumerate(self.groups[0][1])
-        ]
-
-        def body(i, _):
-            self.res[at(place + i)] = self.out1[at(i)]
-            return 0
-
-        lax.fori_loop(0, n, body, 0)
+        self.send(4, [(self.out1, self.res.at[at(place, n)], to) for to, j in self.groups[0][1]])
+        self.res[at(place, n)] = self.out1[...]
 
     def core_back(self):
         n = self.units // 2
         mine = self.base + self.core * n
-        self.flying = [
-            self.copy(29, self.res.at[at(mine, n)], self.res.at[at(mine, n)], core_peer())
-        ]
-
-    def finish(self):
-        for made in self.started:
-            made.wait_send()
-        self.started = []
+        self.send(5, [(self.res.at[at(mine, n)], self.res.at[at(mine, n)], core_peer())])
+
+    def whole(self, phase):
+        first, second = self.units // 16, self.units // 128
+        if phase == 0:
+            return self.core_in
+        if phase == 5:
+            return self.res.at[at(self.base, self.units // 2)]
+        return (self.in1, self.in2, self.out1.at[at(0, 7 * second)], self.res.at[at(self.base, 7 * first)])[phase - 1]
 
 
 class Relay:
-    SEMS = 23
+    SEMS = 5
 
     def __init__(self, src, res, base, units, bufs, sends, recvs):
         self.src, self.res, self.base, self.units = src, res, base, units
@@ -253,7 +245,7 @@
         self.z, self.ring = z_peers()
         self.me, self.group = xy_peers()
         self.core = coords()[3]
-        self.started = []
+        self.done = 0
 
     @staticmethod
     def scratch(units):
@@ -263,7 +255,7 @@
         share = units // 16
         return [block(units // 2), block(units // 2), block(7 * share), block(8 * share), block(share)]
 
-    copy = Stream.copy
+    send = Stream.send
     land = Stream.land
     finish = Stream.finish
     core_out = Stream.core_out
@@ -271,10 +263,10 @@
 
     def scatter1(self):
         n = self.units // 16
-        self.flying = [
-            self.copy(1 + k, self.half.at[at(j * n, n)], self.shares.at[at(k * n, n)], to)
+        self.send(1, [
+            (self.half.at[at(j * n, n)], self.shares.at[at(k * n, n)], to)
             for k, (to, j) in enumerate(self.ring)
-        ]
+        ])
 
     def exchange(self):
         n = self.units // 16
@@ -283,10 +275,7 @@
             total = total + self.shares[at(k * n, n)]
         mine = at(self.me * n, n)
         self.stack[mine] = total
-        self.flying = [
-            self.copy(8 + k, self.stack.at[mine], self.stack.at[mine], to)
-            for k, (to, j) in enumerate(self.group)
-        ]
+        self.send(2, [(self.stack.at[mine], self.stack.at[mine], to) for to, j in self.group])
 
     def gather(self):
         n = self.units // 16
@@ -296,19 +285,24 @@
             total = total + self.stack[at(k * n, n)]
         self.total[...] = total
         self.res[at(place, n)] = total
-        self.flying = [
-            self.copy(15 + k, self.total, self.res.at[at(place, n)], to)
-            for k, (to, j) in enumerate(self.ring)
-        ]
+        self.send(3, [(self.total, self.res.at[at(place, n)], to) for to, j in self.ring])
 
     def core_back(self):
         n = self.units // 2
         mine = at(self.base + self.core * n, n)
-        self.flying = [self.copy(22, self.res.at[mine], self.res.at[mine], core_peer())]
+        self.send(4, [(self.res.at[mine], self.res.at[mine], core_peer())])
+
+    def whole(self, phase):
+        share = self.units // 16
+        if phase == 0:
+            return self.core_in
+        if phase == 4:
+            return self.res.at[at(self.base, self.units // 2)]
+        return (self.shares, self.stack.at[at(0, 7 * share)], self.res.at[at(self.base, 7 * share)])[phase - 1]
 
 
 class Picture:
-    SEMS = 37
+    SEMS = 3
     SHARE = ROWS // 16
 
     def __init__(self, src, res, base, bufs, sends, recvs):
@@ -317,7 +311,7 @@
         self.sends, self.recvs = sends, recvs
         self.me, self.group = flat_peers()
         self.z, self.ring = z_peers()
-        self.started = []
+        self.done = 0
 
     @staticmethod
     def scratch():
@@ -328,16 +322,16 @@
             pltpu.VMEM((n, LANES), F32),
         ]
 
-    copy = Stream.copy
+    send = Stream.send
     land = Stream.land
     finish = Stream.finish
 
     def scatter(self):
         n = self.SHARE
-        self.flying = [
-            self.copy(k, self.src.at[at(self.base + j * n, n)], self.shares.at[at(k * n, n)], to)
+        self.send(0, [
+            (self.src.at[at(self.base + j * n, n)], self.shares.at[at(k * n, n)], to)
             for k, (to, j) in enumerate(self.group)
-        ]
+        ])
 
     def exchange(self):
         n = self.SHARE
@@ -347,10 +341,7 @@
                 total = total + self.shares[at(k * n + i)]
             self.stack[at(self.z * n + i)] = total
         mine = at(self.z * n, n)
-        self.flying = [
-            self.copy(15 + k, self.stack.at[mine], self.stack.at[mine], to)
-            for k, (to, j) in enumerate(self.ring)
-        ]
+        self.send(1, [(self.stack.at[mine], self.stack.at[mine], to) for to, j in self.ring])
 
     def gather(self):
         n = self.SHARE
@@ -362,10 +353,11 @@
             total = total * GAIN
             self.total[at(i)] = total
             self.res[at(place + i)] = total
-        self.flying = [
-            self.copy(22 + k, self.total, self.res.at[at(place, n)], to)
-            for k, (to, j) in enumerate(self.group)
-        ]
+        self.send(2, [(self.total, self.res.at[at(place, n)], to) for to, j in self.group])
+
+    def whole(self, phase):
+        n = self.SHARE
+        return (self.shares, self.stack.at[at(0, 7 * n)], self.res.at[at(self.base, 15 * n)])[phase]
 
 
 def spread(here):
@@ -495,6 +487,13 @@
     for made in loads:
         made.start()
 
+    a0 = Stream(cand, planes, 0, 128, ("xy", "z"), bufs[0:6], sems[0], sems[1])
+    a1 = Stream(cand, planes, 192, 128, ("xy", "z"), bufs[6:12], sems[2], sems[3])
+    b0 = Relay(cand, planes, 128, 64, bufs[12:17], sems[4], sems[5])
+    b1 = Relay(cand, planes, 320, 64, bufs[17:22], sems[6], sems[7])
+    p0 = Picture(images, image_sum, 0, bufs[22:25], sems[8], sems[9])
+    p1 = Picture(images, image_sum, ROWS, bufs[25:28], sems[10], sems[11])
+
     for made in loads[:3] + loads[5:]:
         made.wait()
     omega = omegas[0]
@@ -527,12 +526,6 @@
     lax.fori_loop(0, 8, candidate, 0)
     pl.semaphore_wait(barrier, len(greeted))
 
-    a0 = Stream(cand, planes, 0, 128, ("xy", "z"), bufs[0:6], sems[0], sems[1])
-    a1 = Stream(cand, planes, 192, 128, ("xy", "z"), bufs[6:12], sems[2], sems[3])
-    b0 = Relay(cand, planes, 128, 64, bufs[12:17], sems[4], sems[5])
-    b1 = Relay(cand, planes, 320, 64, bufs[17:22], sems[6], sems[7])
-    p0 = Picture(images, image_sum, 0, bufs[22:25], sems[8], sems[9])
-    p1 = Picture(images, image_sum, ROWS, bufs[25:28], sems[10], sems[11])
     for s in (a0, b0, a1, b1):
         s.core_out()
 
@@ -648,20 +641,21 @@
     a1.core_back()
     lax.fori_loop(20, ROWS // 2, first_step, 0)
     p0.scatter()
-    halo1.wait()
-    spread_rows(field1, nexts, 67 * (1 - tile), HMAX)
     a1.land()
     b1.land()
 
     def second_step(i, _):
-        x = i * 2
+        x = tile * (ROWS - 2) + (1 - 2 * tile) * (i * 2)
         out = two_rows(field1, nexts, planes, coef, 1, x, omega)
         for c in range(4):
             field2[c, at(x, 2)] = out[c]
         images[at(ROWS + x, 2)] = out[0] * out[2] + out[1] * out[3]
         return 0
 
-    lax.fori_loop(0, ROWS // 2, second_step, 0)
+    lax.fori_loop(0, 30, second_step, 0)
+    halo1.wait()
+    spread_rows(field1, nexts, 67 * (1 - tile), HMAX)
+    lax.fori_loop(30, ROWS // 2, second_step, 0)
     p1.scatter()
     p0.land()
     p0.exchange()

time: 67.8 us -> 65.2 us (0.962)
  Pallas kernels: 65 us -> 62.4 us
    pallas_call x1, Pallas kernels: 63.7 us -> 61.1 us  [per_device(): pl.pallas_call(kernel, out_shape=out_shape, in_specs=[hbm] * 10, out_spec...]
where the time goes in v4:
time: 65.2 us; the launch traced here: 65.1 us
  Pallas kernels  62.4 us (96%)
  between operations  1.35 us (2%)
  local copies, waits for them, and re-layouts  1.31 us (2%)
    pallas_call x1, Pallas kernels, per_device(): pl.pallas_call(kernel, out_shape=out_shape, in_specs=[hbm] * 10, out_spec...  61.1 us
    unnamed x8, local copies, waits for them, and re-layouts  1.31 us

profile of v4, /device:TPU:1, one launch (start us, length us, event | category | flops | bytes accessed | tf_op | source)
XLA Modules:
  0.0 65.1 jit_solution(10440898535388455475)
XLA Ops:
  0.6 0.0 copy-start.1
  0.6 0.0 copy-start
  1.3 0.0 copy-done.1
  1.3 0.0 copy-done
  1.3 0.0 copy-start.2
  1.3 0.6 copy-done.2
  2.0 0.0 copy-start.3
  2.0 0.7 %copy-done.3 = s32[4]{0:T(128)S(1)} copy-done((s32[4]{0:T(128)S(1)}, s32[4]{0:T(128)}, u32[]{:S(2)}) %copy-start.3) | copy-done | bytes 40
  2.7 61.1 %migrate.1 = (f32[2,1,64,1024]{3,2,1,0:T(8,128)S(1)}, f32[2,1,64,1024]{3,2,1,0:T(8,128)S(1)}, f32[2,64,1024]{2,1,0:T(8,128)S(1)}) custom-call(f32[1]{0:T(128)S(6)} %copy.13.omegas_in, s32[256]{0:T(256)S(1)} %copy-done, s32[2]{0:T(128)S(1)} %copy-done.1, s32[4]{0:T(128)S(1)} %copy-done.2, s32[4]{0:T(128)S(1)} %copy-done.3, f32[2,1,64,1024]{3,2,1,0:T(8,128)} %source.1, ...), custom_call_target="tpu_custom_call" | custom-call | tf_op jit(solution)/shard_map/migrate/pallas_call | solution.py:730
  63.8 1.3 %hand_over.1 = (f32[2,1,64,1024]{3,2,1,0:T(8,128)}, f32[2,1,64,1024]{3,2,1,0:T(8,128)}, f32[2,64,1024]{2,1,0:T(8,128)}) custom-call(f32[2,1,64,1024]{3,2,1,0:T(8,128)S(1)} %get-tuple-element.6.refs_0_, f32[2,1,64,1024]{3,2,1,0:T(8,128)S(1)} %get-tuple-element.7.refs_1_, f32[2,64,1024]{2,1,0:T(8,128)S(1)} %get-tuple-element.8.refs_2_), custom_call_target="tpu_custom_call" | custom-call | tf_op jit(solution)/shard_map/hand_over/pallas_call | solution.py:763
Async XLA Ops:
  0.6 0.7 %copy-start.1 = (s32[2]{0:T(128)S(1)}, s32[2]{0:T(128)}, u32[]{:S(2)}) copy-start(s32[2]{0:T(128)} %reach_in.1) | copy-start | bytes 28
  0.6 0.7 %copy-start = (s32[256]{0:T(256)S(1)}, s32[256]{0:T(256)}, u32[]{:S(2)}) copy-start(s32[256]{0:T(256)} %owner_in.1) | copy-start | bytes 3076
  1.3 0.7 %copy-start.2 = (s32[4]{0:T(128)S(1)}, s32[4]{0:T(128)}, u32[]{:S(2)}) copy-start(s32[4]{0:T(128)} %srows_in.1) | copy-start | bytes 52
  2.0 0.7 %copy-start.3 = (s32[4]{0:T(128)S(1)}, s32[4]{0:T(128)}, u32[]{:S(2)}) copy-start(s32[4]{0:T(128)} %scols_in.1) | copy-start | bytes 52

commit v5 on v4

--- a/solution.py
+++ b/solution.py
@@ -97,6 +97,11 @@
     return z, [(device(lax.rem(z + k, 8), x, y, c), lax.rem(z + k, 8)) for k in (4, 3, 5, 2, 6, 1, 7)]
 
 
+def x_peers():
+    z, x, y, c = coords()
+    return x, [(device(z, lax.rem(x + k, 4), y, c), lax.rem(x + k, 4)) for k in (2, 1, 3)]
+
+
 def flat_peers():
     z, x, y, c = coords()
     out = []
@@ -236,7 +241,7 @@
 
 
 class Relay:
-    SEMS = 5
+    SEMS = 6
 
     def __init__(self, src, res, base, units, bufs, sends, recvs):
         self.src, self.res, self.base, self.units = src, res, base, units
@@ -244,6 +249,7 @@
         self.sends, self.recvs = sends, recvs
         self.z, self.ring = z_peers()
         self.me, self.group = xy_peers()
+        self.x, self.line = x_peers()
         self.core = coords()[3]
         self.done = 0
 
@@ -253,7 +259,7 @@
             return pltpu.VMEM((n * 8, LANES), F32)
 
         share = units // 16
-        return [block(units // 2), block(units // 2), block(7 * share), block(8 * share), block(share)]
+        return [block(units // 2), block(units // 2), block(7 * share), block(2 * share), block(share)]
 
     send = Stream.send
     land = Stream.land
@@ -268,37 +274,51 @@
             for k, (to, j) in enumerate(self.ring)
         ])
 
-    def exchange(self):
-        n = self.units // 16
+    def scatter2(self):
+        n, quarter = self.units // 16, self.units // 64
         total = self.half[at(self.z * n, n)]
         for k in range(7):
             total = total + self.shares[at(k * n, n)]
-        mine = at(self.me * n, n)
-        self.stack[mine] = total
-        self.send(2, [(self.stack.at[mine], self.stack.at[mine], to) for to, j in self.group])
-
-    def gather(self):
+        self.half[at(self.z * n, n)] = total
+        mine = at(self.me * quarter, quarter)
+        self.stack[mine] = self.half[at(self.z * n + self.x * quarter, quarter)]
+        self.send(2, [
+            (self.half.at[at(self.z * n + lax.div(j, 2) * quarter, quarter)], self.stack.at[mine], to)
+            for to, j in self.group
+        ])
+
+    def gather2(self):
+        quarter = self.units // 64
+        total = self.stack[at(0, quarter)]
+        for k in range(1, 8):
+            total = total + self.stack[at(k * quarter, quarter)]
+        mine = at(self.x * quarter, quarter)
+        self.total[mine] = total
+        self.send(3, [(self.total.at[mine], self.total.at[mine], to) for to, j in self.line])
+
+    def gather1(self):
         n = self.units // 16
         place = self.base + self.core * (self.units // 2) + self.z * n
-        total = self.stack[at(0, n)]
-        for k in range(1, 8):
-            total = total + self.stack[at(k * n, n)]
-        self.total[...] = total
-        self.res[at(place, n)] = total
-        self.send(3, [(self.total, self.res.at[at(place, n)], to) for to, j in self.ring])
+        self.send(4, [(self.total, self.res.at[at(place, n)], to) for to, j in self.ring])
+        self.res[at(place, n)] = self.total[...]
 
     def core_back(self):
         n = self.units // 2
         mine = at(self.base + self.core * n, n)
-        self.send(4, [(self.res.at[mine], self.res.at[mine], core_peer())])
+        self.send(5, [(self.res.at[mine], self.res.at[mine], core_peer())])
 
     def whole(self, phase):
-        share = self.units // 16
+        share, quarter = self.units // 16, self.units // 64
         if phase == 0:
             return self.core_in
-        if phase == 4:
+        if phase == 5:
             return self.res.at[at(self.base, self.units // 2)]
-        return (self.shares, self.stack.at[at(0, 7 * share)], self.res.at[at(self.base, 7 * share)])[phase - 1]
+        return (
+            self.shares,
+            self.stack.at[at(0, 7 * quarter)],
+            self.total.at[at(0, 3 * quarter)],
+            self.res.at[at(self.base, 7 * share)],
+        )[phase - 1]
 
 
 class Picture:
@@ -383,11 +403,17 @@
     lax.fori_loop(0, count, body, 0, unroll=4 if count % 4 == 0 else 1)
 
 
+def plane_unit(step, array, t):
+    if array == 2:
+        return step * 192 + 128 + t * 8
+    return step * 192 + lax.div(t, 4) * 64 + array * 32 + lax.rem(t, 4) * 8
+
+
 def weights_of(planes, step, x, omega):
-    t, s = x // 8, x % 8
+    t, s = lax.div(x, 8), lax.rem(x, 8)
 
     def row(array):
-        start = (step * 3 + array) * 512 + t * 64 + s
+        start = plane_unit(step, array, t) * 8 + s
         both = [planes[pl.ds(start + i, 8, stride=8)] for i in range(2)]
         return jnp.concatenate(both, axis=0)
 
@@ -459,9 +485,9 @@
 
 
 def kernel(
-    omegas_in, owner_in, reach_in, srows_in, scols_in, source, receiver, velocity, epsilon, delta,
+    omegas_in, numbers_in, source, receiver, velocity, epsilon, delta,
     source_out, receiver_out, image_out,
-    omegas, owner, reach, srows, scols,
+    omegas, numbers,
     raw_fields, raw_model, cand, planes, field0, field1, field2, pair1, pair2, pair3, next1, next2,
     next3, coef, images, image_sum, load_sems, halo_sends, halo_recvs, *rest,
 ):
@@ -481,7 +507,7 @@
         loads.append(pltpu.make_async_copy(array, raw_model.at[i], load_sems.at[i]))
     for i, array in enumerate((source, receiver)):
         loads.append(pltpu.make_async_copy(array, raw_fields.at[i], load_sems.at[3 + i]))
-    smalls = ((omegas_in, omegas), (owner_in, owner), (reach_in, reach), (srows_in, srows), (scols_in, scols))
+    smalls = ((omegas_in, omegas), (numbers_in, numbers))
     for i, (array, place) in enumerate(smalls):
         loads.append(pltpu.make_async_copy(array, place, load_sems.at[5 + i]))
     for made in loads:
@@ -497,6 +523,8 @@
     for made in loads[:3] + loads[5:]:
         made.wait()
     omega = omegas[0]
+    owner, reach = [numbers[i] for i in (0, 1)], [numbers[i] for i in (2, 3)]
+    srows, scols = [numbers[4 + i] for i in range(4)], [numbers[8 + i] for i in range(4)]
     picks = []
     for step in range(STEPS):
         for slot in range(2):
@@ -520,7 +548,7 @@
             for step in range(STEPS):
                 for n in range(3):
                     value = picks[step * 2] * forms[0][n] + picks[step * 2 + 1] * forms[1][n]
-                    cand[at((step * 3 + n) * 64 + t * 8 + k)] = value
+                    cand[at(plane_unit(step, n, t) + k)] = value
         return 0
 
     lax.fori_loop(0, 8, candidate, 0)
@@ -582,65 +610,82 @@
         s.scatter1()
     lax.fori_loop(0, 8, arrange, 0)
     halo0 = halo(field0, 0)
+    for s in (a1, b1):
+        s.land()
+        s.core_sum()
+        s.scatter1()
     a0.land()
     a0.sum1_()
     a0.scatter2()
     b0.land()
-    b0.exchange()
-    for s in (a1, b1):
-        s.land()
-        s.core_sum()
-        s.scatter1()
+    b0.scatter2()
     weights()
     spread_rows(field0, pairs, HMAX, ROWS)
+    a1.land()
+    a1.sum1_()
+    a1.scatter2()
+    b1.land()
+    b1.scatter2()
     halo0.wait()
     spread_rows(field0, pairs, 67 * (1 - tile), HMAX)
     a0.land()
     a0.sum2_()
     a0.gather2()
     b0.land()
-    b0.gather()
-    a1.land()
-    a1.sum1_()
-    a1.scatter2()
-    b1.land()
-    b1.exchange()
-    a0.land()
-    a0.gather1()
-    b0.land()
-    b0.core_back()
+    b0.gather2()
     a1.land()
     a1.sum2_()
     a1.gather2()
     b1.land()
-    b1.gather()
-    a0.land()
-    a0.core_back()
-    b0.land()
-    a0.land()
-    a1.land()
-    a1.gather1()
-    b1.land()
-    b1.core_back()
-
-    def first_step(i, _):
-        x = (1 - tile) * (ROWS - 2) + (2 * tile - 1) * (i * 2)
+    b1.gather2()
+    for s in (a0, b0):
+        s.land()
+        s.gather1()
+    for s in (a1, b1):
+        s.land()
+        s.gather1()
+    for s in (a0, b0):
+        s.land()
+        s.core_back()
+
+    core = coords()[3]
+
+    def first_row(i):
+        part = core + lax.div(i, 16) * (1 - 2 * core)
+        return part * 32 + (1 - tile) * 30 + (2 * tile - 1) * (lax.rem(i, 16) * 2)
+
+    def spread_done(i):
+        place = first_row(i) + HMAX
+        for c in range(4):
+            for h in range(2):
+                for pair, value in zip(nexts, spread(field1[c, at(place + h)])):
+                    pair[c, at(place + h)] = value
+
+    def first_pair(i, behind):
+        x = first_row(i)
         out = two_rows(field0, pairs, planes, coef, 0, x, omega)
+        if behind:
+            spread_done(i - 1)
         for c in range(4):
             field1[c, at(x + HMAX, 2)] = out[c]
-            for h in range(2):
-                for pair, value in zip(nexts, spread(out[c][h * 8 : h * 8 + 8])):
-                    pair[c, at(x + HMAX + h)] = value
         images[at(x, 2)] = out[0] * out[2] + out[1] * out[3]
+
+    def first_step(i, _):
+        first_pair(i, True)
         return 0
 
-    lax.fori_loop(0, 2, first_step, 0)
+    first_pair(0, False)
+    lax.fori_loop(1, 16, first_step, 0)
+    for s in (a0, b0):
+        s.land()
+    for s in (a1, b1):
+        s.land()
+        s.core_back()
+    lax.fori_loop(16, 18, first_step, 0)
     halo1 = halo(field1, 1)
-    lax.fori_loop(2, 20, first_step, 0)
-    a1.land()
-    a1.core_back()
-    lax.fori_loop(20, ROWS // 2, first_step, 0)
+    lax.fori_loop(18, ROWS // 2, first_step, 0)
     p0.scatter()
+    spread_done(ROWS // 2 - 1)
     a1.land()
     b1.land()
 
@@ -670,29 +715,30 @@
                 ]
         return 0
 
+    def picture(step):
+        def body(t, _):
+            for k in range(8):
+                place = (pl.ds(pl.multiple_of(t * 8, 8), 8), pl.ds(k * LANES, LANES))
+                image_out[(step,) + place] = image_sum[pl.ds(step * 512 + t * 64 + k, 8, stride=8)]
+            return 0
+
+        return body
+
     lax.fori_loop(0, 8, restore, 0)
     for s in (a0, b0, a1, b1):
         s.finish()
+    p1.land()
+    p1.exchange()
     p0.land()
     p0.gather()
     p1.land()
-    p1.exchange()
+    p1.gather()
+    p0.finish()
+    p0.land()
+    lax.fori_loop(0, 8, picture(0), 0)
+    p1.finish()
     p1.land()
-    p1.gather()
-    for s in (p0, p1):
-        s.finish()
-    p0.land()
-    p1.land()
-
-    def picture(t, _):
-        for step in range(STEPS):
-            for k in range(8):
-                place = (pl.ds(pl.multiple_of(t * 8, 8), 8), pl.ds(k * LANES, LANES))
-                value = image_sum[pl.ds(step * 512 + t * 64 + k, 8, stride=8)]
-                image_out[(step,) + place] = value
-        return 0
-
-    lax.fori_loop(0, 8, picture, 0)
+    lax.fori_loop(0, 8, picture(1), 0)
 
 
 def hand_over(*refs):
@@ -726,13 +772,14 @@
     def small(array):
         return pltpu.SMEM(array.shape, array.dtype)
 
+    numbers = jnp.concatenate([owner[:2], reach, srows, scols])
     counts = [Stream.SEMS] * 4 + [Relay.SEMS] * 4 + [Picture.SEMS] * 4
     made = pl.pallas_call(
         kernel,
         out_shape=out_shape,
-        in_specs=[hbm] * 10,
+        in_specs=[hbm] * 7,
         out_specs=tuple([pl.BlockSpec(memory_space=pltpu.VMEM)] * 3),
-        scratch_shapes=[small(array) for array in (omegas, owner, reach, srows, scols)]
+        scratch_shapes=[small(array) for array in (omegas, numbers)]
         + [
             pltpu.VMEM((2, 2, 1, ROWS, 1024), F32),
             pltpu.VMEM((3, 2, ROWS, 1024), F32),
@@ -759,7 +806,7 @@
             collective_id=0, has_side_effects=True, vmem_limit_bytes=52 << 20
         ),
         name="migrate",
-    )(omegas, owner, reach, srows, scols, source, receiver, velocity, epsilon, delta)
+    )(omegas, numbers, source, receiver, velocity, epsilon, delta)
     return pl.pallas_call(
         hand_over,
         out_shape=out_shape,

time: 65.2 us -> 60.4 us (0.926)
  Pallas kernels: 62.4 us -> 58.2 us
    pallas_call x1, Pallas kernels: 61.1 us -> 56.9 us  [per_device(): pl.pallas_call(kernel, out_shape=out_shape, in_specs=[hbm] * 7, out_specs...]
    unnamed x8 -> x6, local copies, waits for them, and re-layouts: 1.31 us -> 0.65 us
where the time goes in v5:
time: 60.4 us; the launch traced here: 60.3 us
  Pallas kernels  58.2 us (96%)
  between operations  1.34 us (2%)
  local copies, waits for them, and re-layouts  0.66 us (1%)
    pallas_call x1, Pallas kernels, per_device(): pl.pallas_call(kernel, out_shape=out_shape, in_specs=[hbm] * 7, out_specs...  56.9 us
    pallas_call x1, Pallas kernels, per_device(): pl.pallas_call(hand_over, out_shape=out_shape, in_specs=[hbm] * 3, out_sp...  1.3 us

profile of v5, /device:TPU:1, one launch (start us, length us, event | category | flops | bytes accessed | tf_op | source)
XLA Modules:
  0.0 60.3 jit_solution(2910482388040439541)
XLA Ops:
  0.6 0.0 slice-start
  1.3 0.0 copy-start
  1.3 0.0 copy-start.1
  1.3 0.0 copy-start.2
  1.3 0.0 slice-done
  1.3 0.6 %copy-done = s32[4]{0:T(128)S(1)} copy-done((s32[4]{0:T(128)S(1)}, s32[4]{0:T(128)}, u32[]{:S(2)}) %copy-start) | copy-done | bytes 40
  2.0 0.0 copy-done.1
  2.0 0.0 copy-done.2
  2.0 0.1 pad_add_fusion.numbers_in
  2.1 56.9 %migrate.1 = (f32[2,1,64,1024]{3,2,1,0:T(8,128)S(1)}, f32[2,1,64,1024]{3,2,1,0:T(8,128)S(1)}, f32[2,64,1024]{2,1,0:T(8,128)S(1)}) custom-call(f32[1]{0:T(128)S(6)} %copy.13.omegas_in, s32[12]{0:T(128)S(1)} %pad_add_fusion.numbers_in, f32[2,1,64,1024]{3,2,1,0:T(8,128)} %source.1, f32[2,1,64,1024]{3,2,1,0:T(8,128)} %receiver.1, f32[2,64,1024]{2,1,0:T(8,128)} %velocity.1, ...), custom_call_target="tpu_custom_call" | custom-call | tf_op jit(solution)/shard_map/migrate/pallas_call | solution.py:777
  59.0 1.3 %hand_over.1 = (f32[2,1,64,1024]{3,2,1,0:T(8,128)}, f32[2,1,64,1024]{3,2,1,0:T(8,128)}, f32[2,64,1024]{2,1,0:T(8,128)}) custom-call(f32[2,1,64,1024]{3,2,1,0:T(8,128)S(1)} %get-tuple-element.6.refs_0_, f32[2,1,64,1024]{3,2,1,0:T(8,128)S(1)} %get-tuple-element.7.refs_1_, f32[2,64,1024]{2,1,0:T(8,128)S(1)} %get-tuple-element.8.refs_2_), custom_call_target="tpu_custom_call" | custom-call | tf_op jit(solution)/shard_map/hand_over/pallas_call | solution.py:810
Async XLA Ops:
  0.6 0.7 %slice-start = ((s32[256]{0:T(256)}), s32[2]{0:T(128)S(1)}, s32[]{:S(2)}) async-start(s32[256]{0:T(256)} %param.16), calls=%async_computation | async-start | bytes 1024 | tf_op jit(solution)/shard_map/slice | solution.py:775
  1.3 0.7 %copy-start = (s32[4]{0:T(128)S(1)}, s32[4]{0:T(128)}, u32[]{:S(2)}) copy-start(s32[4]{0:T(128)} %param.19) | copy-start | bytes 52
  1.3 0.7 %copy-start.1 = (s32[4]{0:T(128)S(1)}, s32[4]{0:T(128)}, u32[]{:S(2)}) copy-start(s32[4]{0:T(128)} %param.18) | copy-start | bytes 52
  1.3 0.7 %copy-start.2 = (s32[2]{0:T(128)S(1)}, s32[2]{0:T(128)}, u32[]{:S(2)}) copy-start(s32[2]{0:T(128)} %param.17) | copy-start | bytes 28

commit v6 on v5

--- a/solution.py
+++ b/solution.py
@@ -400,7 +400,7 @@
                 pair[c, at(first + i)] = value
         return 0
 
-    lax.fori_loop(0, count, body, 0, unroll=4 if count % 4 == 0 else 1)
+    lax.fori_loop(0, count, body, 0, unroll=4 if count % 4 == 0 else count)
 
 
 def plane_unit(step, array, t):
@@ -444,29 +444,29 @@
     return turn, g
 
 
-def two_rows(field, pairs, planes, coef, step, x, omega):
+def gathered(field, pairs, x, r, c):
     rows = [field] + list(pairs)
-
-    def gathered(r, c):
-        total = None
-        for a in range(4):
-            for b in range(4):
-                if a * a + b * b != r:
-                    continue
-                for shift in sorted({a, -a}):
-                    piece = rows[b][c, at(x + HMAX + shift, 2)]
-                    total = piece if total is None else total + piece
-        return total
-
+    total = None
+    for a in range(4):
+        for b in range(4):
+            if a * a + b * b != r:
+                continue
+            for shift in sorted({a, -a}):
+                piece = rows[b][c, at(x + HMAX + shift, 2)]
+                total = piece if total is None else total + piece
+    return total
+
+
+def two_rows(sums, planes, coef, step, x, omega):
     turn, g = weights_of(planes, step, x, omega)
     first = coef[at(step * 20, 2)]
-    acc = [first * gathered(0, c) for c in range(4)]
+    acc = [first * sums(0, c) for c in range(4)]
     for index, r in enumerate(GROUPS):
         if r == 0:
             continue
         scale = coef[at(step * 20 + index * 2, 2)]
         wr, wi = g[r][0] * scale, g[r][1] * scale
-        sr, si, rr, ri = [gathered(r, c) for c in range(4)]
+        sr, si, rr, ri = [sums(r, c) for c in range(4)]
         acc[0] = acc[0] + (wr * sr - wi * si)
         acc[1] = acc[1] + (wr * si + wi * sr)
         acc[2] = acc[2] + (wr * rr + wi * ri)
@@ -489,7 +489,7 @@
     source_out, receiver_out, image_out,
     omegas, numbers,
     raw_fields, raw_model, cand, planes, field0, field1, field2, pair1, pair2, pair3, next1, next2,
-    next3, coef, images, image_sum, load_sems, halo_sends, halo_recvs, *rest,
+    next3, kept, coef, images, image_sum, load_sems, halo_sends, halo_recvs, *rest,
 ):
     sems, bufs = rest[:12], rest[12:]
     tile = lax.axis_index("tile")
@@ -644,6 +644,14 @@
     for s in (a1, b1):
         s.land()
         s.gather1()
+
+    def keep(i, _):
+        for index, r in enumerate(GROUPS):
+            for c in range(4):
+                kept[index * 4 + c, at(i * 2, 2)] = gathered(field0, pairs, i * 2, r, c)
+        return 0
+
+    lax.fori_loop(0, ROWS // 2, keep, 0)
     for s in (a0, b0):
         s.land()
         s.core_back()
@@ -663,7 +671,7 @@
 
     def first_pair(i, behind):
         x = first_row(i)
-        out = two_rows(field0, pairs, planes, coef, 0, x, omega)
+        out = two_rows(lambda r, c: kept[GROUPS.index(r) * 4 + c, at(x, 2)], planes, coef, 0, x, omega)
         if behind:
             spread_done(i - 1)
         for c in range(4):
@@ -691,7 +699,7 @@
 
     def second_step(i, _):
         x = tile * (ROWS - 2) + (1 - 2 * tile) * (i * 2)
-        out = two_rows(field1, nexts, planes, coef, 1, x, omega)
+        out = two_rows(lambda r, c: gathered(field1, nexts, x, r, c), planes, coef, 1, x, omega)
         for c in range(4):
             field2[c, at(x, 2)] = out[c]
         images[at(ROWS + x, 2)] = out[0] * out[2] + out[1] * out[3]
@@ -742,14 +750,14 @@
 
 
 def hand_over(*refs):
-    between, sems = refs[6:9], refs[9]
-    loads = [pltpu.make_async_copy(refs[i], between[i], sems.at[i]) for i in range(3)]
-    stores = [pltpu.make_async_copy(between[i], refs[3 + i], sems.at[3 + i]) for i in range(3)]
-    for made in loads:
+    sems = refs[6]
+    stores = [
+        pltpu.make_async_copy(refs[i].at[h], refs[3 + i].at[h], sems.at[i * 2 + h])
+        for i in range(3)
+        for h in range(2)
+    ]
+    for made in stores:
         made.start()
-    for load, store in zip(loads, stores):
-        load.wait()
-        store.start()
     for made in stores:
         made.wait()
 
@@ -791,6 +799,7 @@
         ]
         + [plane(TALL)] * 6
         + [
+            pltpu.VMEM((4 * len(GROUPS), ROWS * 8, LANES), F32),
             block(40),
             block(IMAGE_UNITS),
             block(IMAGE_UNITS),
@@ -810,10 +819,9 @@
     return pl.pallas_call(
         hand_over,
         out_shape=out_shape,
-        in_specs=[hbm] * 3,
+        in_specs=[pl.BlockSpec(memory_space=pltpu.VMEM)] * 3,
         out_specs=(hbm, hbm, hbm),
-        scratch_shapes=[pltpu.VMEM(o.shape, F32) for o in out_shape]
-        + [pltpu.SemaphoreType.DMA((6,))],
+        scratch_shapes=[pltpu.SemaphoreType.DMA((6,))],
         compiler_params=pltpu.CompilerParams(vmem_limit_bytes=52 << 20),
         name="hand_over",
     )(*made)

time: 60.4 us -> 59.7 us (0.988)
  Pallas kernels: 58.2 us -> 57.5 us
    pallas_call x1, Pallas kernels: 56.9 us -> 56.3 us  [per_device(): pl.pallas_call(kernel, out_shape=out_shape, in_specs=[hbm] * 7, out_specs...]
where the time goes in v6:
time: 59.7 us; the launch traced here: 59.5 us
  Pallas kernels  57.5 us (96%)
  between operations  1.34 us (2%)
  local copies, waits for them, and re-layouts  0.66 us (1%)
    pallas_call x1, Pallas kernels, per_device(): pl.pallas_call(kernel, out_shape=out_shape, in_specs=[hbm] * 7, out_specs...  56.3 us

profile of v6, /device:TPU:1, one launch (start us, length us, event | category | flops | bytes accessed | tf_op | source)
XLA Modules:
  0.0 59.5 jit_solution(2950652566902297955)
XLA Ops:
  0.6 0.0 slice-start
  1.3 0.0 copy-start
  1.3 0.0 copy-start.1
  1.3 0.0 copy-start.2
  1.3 0.0 slice-done
  1.3 0.6 %copy-done = s32[4]{0:T(128)S(1)} copy-done((s32[4]{0:T(128)S(1)}, s32[4]{0:T(128)}, u32[]{:S(2)}) %copy-start) | copy-done | bytes 40
  2.0 0.0 copy-done.1
  2.0 0.0 copy-done.2
  2.0 0.1 pad_add_fusion.numbers_in
  2.1 56.3 %migrate.1 = (f32[2,1,64,1024]{3,2,1,0:T(8,128)S(1)}, f32[2,1,64,1024]{3,2,1,0:T(8,128)S(1)}, f32[2,64,1024]{2,1,0:T(8,128)S(1)}) custom-call(f32[1]{0:T(128)S(6)} %copy.13.omegas_in, s32[12]{0:T(128)S(1)} %pad_add_fusion.numbers_in, f32[2,1,64,1024]{3,2,1,0:T(8,128)} %source.1, f32[2,1,64,1024]{3,2,1,0:T(8,128)} %receiver.1, f32[2,64,1024]{2,1,0:T(8,128)} %velocity.1, ...), custom_call_target="tpu_custom_call" | custom-call | tf_op jit(solution)/shard_map/migrate/pallas_call | solution.py:785
  58.4 1.2 %hand_over.1 = (f32[2,1,64,1024]{3,2,1,0:T(8,128)}, f32[2,1,64,1024]{3,2,1,0:T(8,128)}, f32[2,64,1024]{2,1,0:T(8,128)}) custom-call(f32[2,1,64,1024]{3,2,1,0:T(8,128)S(1)} %get-tuple-element.6.refs_0_, f32[2,1,64,1024]{3,2,1,0:T(8,128)S(1)} %get-tuple-element.7.refs_1_, f32[2,64,1024]{2,1,0:T(8,128)S(1)} %get-tuple-element.8.refs_2_), custom_call_target="tpu_custom_call" | custom-call | tf_op jit(solution)/shard_map/hand_over/pallas_call | solution.py:819
Async XLA Ops:
  0.6 0.7 %slice-start = ((s32[256]{0:T(256)}), s32[2]{0:T(128)S(1)}, s32[]{:S(2)}) async-start(s32[256]{0:T(256)} %param.16), calls=%async_computation | async-start | bytes 1024 | tf_op jit(solution)/shard_map/slice | solution.py:783
  1.3 0.7 %copy-start = (s32[4]{0:T(128)S(1)}, s32[4]{0:T(128)}, u32[]{:S(2)}) copy-start(s32[4]{0:T(128)} %param.19) | copy-start | bytes 52
  1.3 0.7 %copy-start.1 = (s32[4]{0:T(128)S(1)}, s32[4]{0:T(128)}, u32[]{:S(2)}) copy-start(s32[4]{0:T(128)} %param.18) | copy-start | bytes 52
  1.3 0.7 %copy-start.2 = (s32[2]{0:T(128)S(1)}, s32[2]{0:T(128)}, u32[]{:S(2)}) copy-start(s32[2]{0:T(128)} %param.17) | copy-start | bytes 28

commit v7 on v6

--- a/solution.py
+++ b/solution.py
@@ -792,17 +792,17 @@
             pltpu.VMEM((2, 2, 1, ROWS, 1024), F32),
             pltpu.VMEM((3, 2, ROWS, 1024), F32),
             block(PLANE_UNITS),
-            block(PLANE_UNITS),
+            block(PLANE_UNITS + 1),
             plane(TALL),
             plane(TALL),
-            plane(ROWS),
+            plane(ROWS + 1),
         ]
         + [plane(TALL)] * 6
         + [
             pltpu.VMEM((4 * len(GROUPS), ROWS * 8, LANES), F32),
             block(40),
             block(IMAGE_UNITS),
-            block(IMAGE_UNITS),
+            block(IMAGE_UNITS + 1),
             pltpu.SemaphoreType.DMA((10,)),
             pltpu.SemaphoreType.DMA((2,)),
             pltpu.SemaphoreType.DMA((2,)),

time: 59.7 us -> 59.7 us (level)
  no operation moved by 1% of the time
where the time goes in v7:
time: 59.7 us; the launch traced here: 59.6 us
  Pallas kernels  57.5 us (96%)
  between operations  1.34 us (2%)
  local copies, waits for them, and re-layouts  0.66 us (1%)
    pallas_call x1, Pallas kernels, per_device(): pl.pallas_call(kernel, out_shape=out_shape, in_specs=[hbm] * 7, out_specs...  56.3 us

profile of v7, /device:TPU:1, one launch (start us, length us, event | category | flops | bytes accessed | tf_op | source)
XLA Modules:
  0.0 59.6 jit_solution(8613586114151155788)
XLA Ops:
  0.6 0.0 slice-start
  1.3 0.0 copy-start
  1.3 0.0 copy-start.1
  1.3 0.0 copy-start.2
  1.3 0.0 slice-done
  1.3 0.6 %copy-done = s32[4]{0:T(128)S(1)} copy-done((s32[4]{0:T(128)S(1)}, s32[4]{0:T(128)}, u32[]{:S(2)}) %copy-start) | copy-done | bytes 40
  2.0 0.0 copy-done.1
  2.0 0.0 copy-done.2
  2.0 0.1 pad_add_fusion.numbers_in
  2.1 56.3 %migrate.1 = (f32[2,1,64,1024]{3,2,1,0:T(8,128)S(1)}, f32[2,1,64,1024]{3,2,1,0:T(8,128)S(1)}, f32[2,64,1024]{2,1,0:T(8,128)S(1)}) custom-call(f32[1]{0:T(128)S(6)} %copy.13.omegas_in, s32[12]{0:T(128)S(1)} %pad_add_fusion.numbers_in, f32[2,1,64,1024]{3,2,1,0:T(8,128)} %source.1, f32[2,1,64,1024]{3,2,1,0:T(8,128)} %receiver.1, f32[2,64,1024]{2,1,0:T(8,128)} %velocity.1, ...), custom_call_target="tpu_custom_call" | custom-call | tf_op jit(solution)/shard_map/migrate/pallas_call | solution.py:785
  58.4 1.2 %hand_over.1 = (f32[2,1,64,1024]{3,2,1,0:T(8,128)}, f32[2,1,64,1024]{3,2,1,0:T(8,128)}, f32[2,64,1024]{2,1,0:T(8,128)}) custom-call(f32[2,1,64,1024]{3,2,1,0:T(8,128)S(1)} %get-tuple-element.6.refs_0_, f32[2,1,64,1024]{3,2,1,0:T(8,128)S(1)} %get-tuple-element.7.refs_1_, f32[2,64,1024]{2,1,0:T(8,128)S(1)} %get-tuple-element.8.refs_2_), custom_call_target="tpu_custom_call" | custom-call | tf_op jit(solution)/shard_map/hand_over/pallas_call | solution.py:819
Async XLA Ops:
  0.6 0.7 %slice-start = ((s32[256]{0:T(256)}), s32[2]{0:T(128)S(1)}, s32[]{:S(2)}) async-start(s32[256]{0:T(256)} %param.16), calls=%async_computation | async-start | bytes 1024 | tf_op jit(solution)/shard_map/slice | solution.py:783
  1.3 0.7 %copy-start = (s32[4]{0:T(128)S(1)}, s32[4]{0:T(128)}, u32[]{:S(2)}) copy-start(s32[4]{0:T(128)} %param.19) | copy-start | bytes 52
  1.3 0.7 %copy-start.1 = (s32[4]{0:T(128)S(1)}, s32[4]{0:T(128)}, u32[]{:S(2)}) copy-start(s32[4]{0:T(128)} %param.18) | copy-start | bytes 52
  1.3 0.7 %copy-start.2 = (s32[2]{0:T(128)S(1)}, s32[2]{0:T(128)}, u32[]{:S(2)}) copy-start(s32[2]{0:T(128)} %param.17) | copy-start | bytes 28
